TPU v7x, 32 devices: a whole 2x2x4 slice. The times are simulated.
32 devices in a mesh: grp: 4 (over y, core), mem: 8 (over z, x).
Axes of the slice: x: 2, y: 2, z: 4, core: 2. Of those that a mesh axis runs over, the one named last changes fastest.
Arguments:
- spectral: bfloat16 [512, 3, 2, 256, 192], P('grp', None, None, 'mem'), may hold values from -6 to 6
- inverse: bfloat16 [512, 48, 192], P('grp'), may hold values from -0.4375 to 0.4375
- legendre: bfloat16 [256, 64, 512], P('mem', None, 'grp'), may hold values from -0.015625 to 0.015625
- vorticity: bfloat16 [3, 64, 48, 1536], P(None, 'mem', 'grp'), may hold values from -6 to 6
- degree_list: int32 [512], replicated, may hold values from 0 to 511, as said below
- order_map: int32 [256], replicated, may hold values from 0 to 255, as said below
Outputs:
- advection: bfloat16 [3, 64, 48, 1536], P(None, 'mem', 'grp')
Inputs may be any that keep to these rules, and one draw needn't show every extreme that they name: `degree_list`: a permutation of the degrees; slots 2j and 2j + 1 hold a degree d and 511 - d. `order_map`: a permutation of the orders; slots 2j and 2j + 1 hold an order m and 255 - m.
All inputs are finite; a program needn't handle non-finite values.
Results may differ from a plain program's by a relative error of at most 0.0062.
Values may be sent and summed in bfloat16 or wider, within the bound.
A program may use at most 64 MiB of HBM per device.

v0:
```python
import math

import jax
import jax.numpy as jnp
from jax import lax
from jax.sharding import PartitionSpec as P


def cross_product(flow_velocity, vorticity):
    other = vorticity.astype(jnp.float32)
    first = flow_velocity[:, :, 1] * other[2] - flow_velocity[:, :, 2] * other[1]
    second = flow_velocity[:, :, 2] * other[0] - flow_velocity[:, :, 0] * other[2]
    third = flow_velocity[:, :, 0] * other[1] - flow_velocity[:, :, 1] * other[0]
    return jnp.stack([first, second, third]).astype(jnp.bfloat16)


def fourier_table(order_map, count):
    longitude = jnp.arange(count, dtype=jnp.int32)
    phase = order_map[:, None] * longitude[None, :] % count
    angle = phase.astype(jnp.float32) * (2.0 * math.pi / count)
    weight = jnp.where(order_map == 0, 1.0, 2.0).astype(jnp.float32)[:, None]
    return jnp.stack([weight * jnp.cos(angle), -weight * jnp.sin(angle)], axis=1).astype(
        jnp.bfloat16
    )


def solve_radial(rows, profiles):
    width_now = profiles.shape[0]
    orders_here = profiles.shape[3]
    flat_profiles = profiles.reshape(width_now, 6 * orders_here, profiles.shape[4])
    solved = lax.dot_general(
        rows, flat_profiles, (((2,), (2,)), ((0,), (0,))), preferred_element_type=jnp.float32
    )
    return solved.astype(jnp.bfloat16)


def order_major(values, orders_here):
    width_now = values.shape[0]
    shells_now = values.shape[1]
    return jnp.transpose(values.reshape(width_now, shells_now * 6, orders_here), (2, 0, 1))


def legendre_term(segment, block, degree_list, local_order_list):
    allowed = local_order_list[:, None] <= degree_list[None, :]
    table = jnp.where(allowed[:, None, :], segment, jnp.zeros_like(segment))
    product = lax.dot_general(
        table, block, (((2,), (1,)), ((0,), (0,))), preferred_element_type=jnp.float32
    )
    return product


def shards(spectral, inverse, legendre, vorticity, degree_list, order_map):
    member_order_list = spectral.shape[3]
    member_shell_rows = vorticity.shape[2]
    member_index = lax.axis_index("mem")
    local_order_list = lax.dynamic_slice_in_dim(
        order_map, member_index * member_order_list, member_order_list
    )
    radial_factor = solve_radial(inverse, spectral)
    moved = lax.all_to_all(radial_factor, "grp", split_axis=1, concat_axis=0, tiled=True)
    by_order = order_major(moved, member_order_list)
    merged_value_rows = legendre_term(
        lax.all_gather(legendre, "grp", axis=2, tiled=True), by_order, degree_list, local_order_list
    )
    latitudinal = merged_value_rows.astype(jnp.bfloat16)
    gathered = lax.all_to_all(latitudinal, "mem", split_axis=1, concat_axis=0, tiled=True)
    complete_order_list = gathered.shape[0]
    member_latitude_rows = gathered.shape[1]
    arranged = gathered.reshape(complete_order_list, member_latitude_rows, member_shell_rows, 3, 2)
    trig = fourier_table(order_map, vorticity.shape[3])
    flow_velocity = jnp.einsum(
        "mtsck,mkp->tscp", arranged, trig, preferred_element_type=jnp.float32
    )
    return cross_product(flow_velocity, vorticity)


def solution(mesh):
    return jax.shard_map(
        shards,
        mesh=mesh,
        in_specs=(
            P("grp", None, None, "mem", None),
            P("grp", None, None),
            P("mem", None, "grp"),
            P(None, "mem", "grp", None),
            P(),
            P(),
        ),
        out_specs=P(None, "mem", "grp", None),
        check_vma=False,
    )
```

profile of v0, /device:TPU:0, one launch (start us, length us, event | category | flops | bytes accessed | tf_op | source)
XLA Modules:
  0.0 120.3 jit_solution(7360711540219282425)
XLA Ops:
  6.5 0.0 all-gather.2.cloned.1.call-start
  6.5 0.7 all-gather.2.cloned.1.call-update
  7.3 0.0 copy-start.1
  7.3 17.6 %copy.25 = bf16[128,192,192]{2,1,0:T(8,128)(2,1)} copy(bf16[128,192,192]{0,2,1:T(8,128)(2,1)} %bitcast.50) | data formatting | bytes 18874368 | tf_op jit(solution)/shard_map/reshape | solution.py:30
  24.9 0.0 copy-done.1
  24.9 3.5 %copy.24 = bf16[128,48,192]{2,1,0:T(8,128)(2,1)} copy(bf16[128,48,192]{0,2,1:T(8,128)(2,1)S(1)} %copy-done.1) | data formatting | bytes 4718592 | tf_op args[1]
  28.4 9.6 %convolution_convert_fusion = bf16[128,48,192]{2,1,0:T(8,128)(2,1)S(1)} fusion(bf16[128,48,192]{2,1,0:T(8,128)(2,1)} %copy.24, bf16[128,192,192]{2,1,0:T(8,128)(2,1)} %copy.25), kind=kOutput, calls=%fused_computation.5 | convolution fusion | flops 454164480 | bytes 14155776 | tf_op jit(solution)/shard_map/dot_general | solution.py:31
  38.0 3.4 %copy.26 = bf16[128,48,192]{0,2,1:T(8,128)(2,1)} copy(bf16[128,48,192]{2,1,0:T(8,128)(2,1)S(1)} %convolution_convert_fusion) | data formatting | bytes 4718592 | tf_op jit(solution)/shard_map/convert_element_type | solution.py:34
  41.4 0.0 copy-start.3
  41.4 0.0 copy-start.4
  41.4 0.0 copy-start.2
  41.4 4.5 %all-to-all-start = ((bf16[128,48,192]{0,2,1:T(8,128)(2,1)}), bf16[128,48,192]{0,2,1:T(8,128)(2,1)S(1)}, u32[]{:S(2)}, u32[]{:S(2)}) async-start(bf16[128,48,192]{0,2,1:T(8,128)(2,1)} %copy.26), calls=%async_computation | async-start | bytes 4718592 | tf_op jit(solution)/shard_map/all_to_all | solution.py:60
  45.9 0.0 copy-done.3
  45.9 0.1 dynamic_slice.3
  46.0 0.0 copy-done.4
  46.0 0.1 broadcast_compare_fusion
  46.0 0.0 copy-done.2
  46.0 1.8 %copy_convert_fusion = f32[3,8,12,1536]{3,2,1,0:T(8,128)} fusion(bf16[3,8,12,1536]{3,1,2,0:T(8,128)(2,1)S(1)} %copy-done.2), kind=kLoop, calls=%fused_computation.21 | loop fusion | flops 442368 | bytes 2654208 | tf_op jit(solution)/shard_map/convert_element_type | solution.py:10
  47.9 26.5 %all-to-all-done = bf16[128,48,192]{0,2,1:T(8,128)(2,1)S(1)} async-done(((bf16[128,48,192]{0,2,1:T(8,128)(2,1)}), bf16[128,48,192]{0,2,1:T(8,128)(2,1)S(1)}, u32[]{:S(2)}, u32[]{:S(2)}) %all-to-all-start) | async-done | bytes 2359328 | tf_op jit(solution)/shard_map/all_to_all | solution.py:60
  74.4 3.2 %copy.27 = bf16[4,128,12,192]{1,0,3,2:T(4,128)(2,1)} copy(bf16[4,128,12,192]{1,3,2,0:T(8,128)(2,1)S(1)} %bitcast.49) | data formatting | bytes 4718592 | tf_op jit(solution)/shard_map/all_to_all | solution.py:60
  77.6 4.0 %reshape.160 = bf16[512,72,32]{0,2,1:T(8,128)(2,1)S(1)} reshape(bf16[4,128,12,192]{1,0,3,2:T(4,128)(2,1)} %copy.27) | data formatting | bytes 4718592 | tf_op jit(solution)/shard_map/reshape | solution.py:40
  81.7 0.0 all-gather.2.cloned.1.call-done
  81.7 3.2 %fusion.12 = bf16[32,64,72]{2,1,0:T(8,128)(2,1)S(1)} fusion(bf16[512,72,32]{0,2,1:T(8,128)(2,1)S(1)} %reshape.160, bf16[32,64,512]{2,1,0:T(8,128)(2,1)} %all-gather.2.cloned.1.call-done, pred[32,512]{1,0:T(8,128)(4,1)S(1)} %broadcast_compare_fusion), kind=kOutput, calls=%fused_computation.19 | convolution fusion | flops 152190976 | bytes 4767744 | tf_op jit(solution)/shard_map/dot_general | solution.py:46
  84.9 1.1 copy.29
  86.0 6.6 %all-to-all-start.1 = ((bf16[32,64,72]{2,0,1:T(8,128)(2,1)}), bf16[32,64,72]{2,0,1:T(8,128)(2,1)S(1)}, u32[]{:S(2)}, u32[]{:S(2)}) async-start(bf16[32,64,72]{2,0,1:T(8,128)(2,1)} %copy.29), calls=%async_computation.1 | async-start | bytes 1048576 | tf_op jit(solution)/shard_map/all_to_all | solution.py:66
  92.6 7.2 %multiply_convert_fusion.1 = (bf16[256,1,1536]{2,0,1:T(8,128)(2,1)S(1)}, bf16[256,1,1536]{2,0,1:T(8,128)(2,1)S(1)}) fusion(s32[256]{0:T(256)S(1)} %copy-done.3, f32[256]{0:T(256)S(1)} %get-tuple-element.10, f32[256]{0:T(256)S(1)} %get-tuple-element.11), kind=kLoop, calls=%fused_computation.14 | loop fusion | flops 5111808 | bytes 1575936 | tf_op jit(solution)/shard_map/convert.3
  99.8 7.1 %all-to-all-done.1 = bf16[32,64,72]{2,0,1:T(8,128)(2,1)S(1)} async-done(((bf16[32,64,72]{2,0,1:T(8,128)(2,1)}), bf16[32,64,72]{2,0,1:T(8,128)(2,1)S(1)}, u32[]{:S(2)}, u32[]{:S(2)}) %all-to-all-start.1) | async-done | bytes 294944 | tf_op jit(solution)/shard_map/all_to_all | solution.py:66
  106.9 1.8 %copy.30 = bf16[32,8,8,72]{0,1,2,3:T(8,128)(2,1)S(1)} copy(bf16[32,8,8,72]{3,0,2,1:T(8,128)(2,1)S(1)} %bitcast.52) | data formatting | bytes 589824 | tf_op jit(solution)/shard_map/all_to_all | solution.py:66
  108.7 0.8 reshape.161
  109.5 0.0 copy-start
  109.6 0.8 convolution_bitcast_fusion
  110.3 0.9 copy-done
  111.2 0.6 subtract_convert_fusion.2
  111.8 0.2 pad_maximum_fusion
  112.0 1.4 %copy.35 = bf16[3,8,12,1536]{3,1,2,0:T(8,128)(2,1)} copy(bf16[3,8,12,1536]{3,2,1,0:T(8,128)(2,1)S(1)} %pad_maximum_fusion) | data formatting | bytes 1769472 | tf_op jit(solution)/shard_map/stack | solution.py:14
  (1 shorter events, 0.0 us)
Async XLA Ops:
  6.5 75.1 %all-gather.2.cloned.1.call-start = ((), (), s32[]{:S(2)}) async-start(), calls=%async_computation.2 | async-start | bytes 2621440 | tf_op jit(solution)/shard_map/all_gather | solution.py:63
  7.3 17.6 %copy-start.1 = (bf16[128,48,192]{0,2,1:T(8,128)(2,1)S(1)}, bf16[128,48,192]{0,2,1:T(8,128)(2,1)}, u32[]{:S(2)}) copy-start(bf16[128,48,192]{0,2,1:T(8,128)(2,1)} %param.7) | copy-start | bytes 7077892
  41.4 4.5 %copy-start.3 = (s32[256]{0:T(256)S(1)}, s32[256]{0:T(256)}, u32[]{:S(2)}) copy-start(s32[256]{0:T(256)} %param.11) | copy-start | bytes 3076
  41.4 4.6 %copy-start.4 = (s32[512]{0:T(512)S(1)}, s32[512]{0:T(512)}, u32[]{:S(2)}) copy-start(s32[512]{0:T(512)} %param.10) | copy-start | bytes 6148
  41.4 4.6 %copy-start.2 = (bf16[3,8,12,1536]{3,1,2,0:T(8,128)(2,1)S(1)}, bf16[3,8,12,1536]{3,1,2,0:T(8,128)(2,1)}, u32[]{:S(2)}) copy-start(bf16[3,8,12,1536]{3,1,2,0:T(8,128)(2,1)} %param.9) | copy-start | bytes 2654212
  41.4 33.0 %all-to-all-start = ((bf16[128,48,192]{0,2,1:T(8,128)(2,1)}), bf16[128,48,192]{0,2,1:T(8,128)(2,1)S(1)}, u32[]{:S(2)}, u32[]{:S(2)}) async-start(bf16[128,48,192]{0,2,1:T(8,128)(2,1)} %copy.26), calls=%async_computation | async-start | bytes 4718592 | tf_op jit(solution)/shard_map/all_to_all | solution.py:60
  86.0 20.9 %all-to-all-start.1 = ((bf16[32,64,72]{2,0,1:T(8,128)(2,1)}), bf16[32,64,72]{2,0,1:T(8,128)(2,1)S(1)}, u32[]{:S(2)}, u32[]{:S(2)}) async-start(bf16[32,64,72]{2,0,1:T(8,128)(2,1)} %copy.29), calls=%async_computation.1 | async-start | bytes 1048576 | tf_op jit(solution)/shard_map/all_to_all | solution.py:66
  109.5 1.7 %copy-start = (f32[3,8,12,1536]{3,2,1,0:T(8,128)S(1)}, f32[3,8,12,1536]{3,2,1,0:T(8,128)}, u32[]{:S(2)}) copy-start(f32[3,8,12,1536]{3,2,1,0:T(8,128)} %copy_convert_fusion) | copy-start | bytes 5308420
Sparse Core Ops, SparseCore 0:
  8.9 25.5 all-gather.1
where the time goes:
time: 121 us; the launch traced here: 120 us
  local copies, waits for them, and re-layouts  37.8 us (31%)
  waiting for transfers between devices  34.3 us (28%)
  matrix products  13.6 us (11%)
  between operations  13.5 us (11%)
  starting transfers between devices  11.1 us (9%)
  other arithmetic  9.91 us (8%)
    all_to_all x1, waiting for transfers between devices, shards(): lax.all_to_all(radial_factor, 'grp', split_axis=1, concat_axis=0, tiled=T...  26.5 us
    reshape x1, local copies, waits for them, and re-layouts, solve_radial(): profiles.reshape(width_now, 6 * orders_here, profiles.shape[4])  17.6 us
    dot_general x1, matrix products, solve_radial(): lax.dot_general(rows, flat_profiles, (((2,), (2,)), ((0,), (0,))), prefer...  9.62 us
    another operation x2, other arithmetic  7.84 us
    all_to_all x1, waiting for transfers between devices, shards(): lax.all_to_all(latitudinal, 'mem', split_axis=1, concat_axis=0, tiled=True)  7.09 us
    all_to_all x1, starting transfers between devices, shards(): lax.all_to_all(latitudinal, 'mem', split_axis=1, concat_axis=0, tiled=True)  6.62 us
    all_to_all x1, starting transfers between devices, shards(): lax.all_to_all(radial_factor, 'grp', split_axis=1, concat_axis=0, tiled=T...  4.48 us
    unnamed x11, local copies, waits for them, and re-layouts  4.41 us
  transfers between devices with their start and end apart: 3, of which 2 were waited for; matrix products, arithmetic and copies ran while one was open for 42% of the time, Pallas kernels for 0%

commit v1 on v0

v1 whole, which is shorter than its diff:
```python
import functools
import math

import jax
import jax.numpy as jnp
from jax import lax
from jax.experimental import pallas as pl
from jax.experimental.pallas import tpu as pltpu
from jax.sharding import PartitionSpec as P

F32 = jnp.float32
BF16 = jnp.bfloat16
LANES = 128
NT = (((1,), (1,)), ((), ()))
NN = (((1,), (0,)), ((), ()))


def nt(a, b):
    return lax.dot_general(a, b, NT, preferred_element_type=F32)


def nn(a, b):
    return lax.dot_general(a, b, NN, preferred_element_type=F32)


def cross_product(flow_velocity, vorticity):
    other = vorticity.astype(jnp.float32)
    first = flow_velocity[:, :, 1] * other[2] - flow_velocity[:, :, 2] * other[1]
    second = flow_velocity[:, :, 2] * other[0] - flow_velocity[:, :, 0] * other[2]
    third = flow_velocity[:, :, 0] * other[1] - flow_velocity[:, :, 1] * other[0]
    return jnp.stack([first, second, third]).astype(jnp.bfloat16)


def fourier_table(order_map, count):
    longitude = jnp.arange(count, dtype=jnp.int32)
    phase = order_map[:, None] * longitude[None, :] % count
    angle = phase.astype(jnp.float32) * (2.0 * math.pi / count)
    weight = jnp.where(order_map == 0, 1.0, 2.0).astype(jnp.float32)[:, None]
    return jnp.stack([weight * jnp.cos(angle), -weight * jnp.sin(angle)], axis=1).astype(
        jnp.bfloat16
    )


def plain_shards(spectral, inverse, legendre, vorticity, degree_list, order_map):
    orders = spectral.shape[3]
    shells = vorticity.shape[2]
    local_order_list = lax.dynamic_slice_in_dim(
        order_map, lax.axis_index("mem") * orders, orders
    )
    width = spectral.shape[0]
    flat = spectral.reshape(width, 6 * orders, spectral.shape[4])
    solved = lax.dot_general(
        inverse, flat, (((2,), (2,)), ((0,), (0,))), preferred_element_type=F32
    ).astype(BF16)
    moved = lax.all_to_all(solved, "grp", split_axis=1, concat_axis=0, tiled=True)
    by_order = jnp.transpose(
        moved.reshape(moved.shape[0], moved.shape[1] * 6, orders), (2, 0, 1)
    )
    segment = lax.all_gather(legendre, "grp", axis=2, tiled=True)
    allowed = local_order_list[:, None] <= degree_list[None, :]
    table = jnp.where(allowed[:, None, :], segment, jnp.zeros_like(segment))
    latitudinal = lax.dot_general(
        table, by_order, (((2,), (1,)), ((0,), (0,))), preferred_element_type=F32
    ).astype(BF16)
    gathered = lax.all_to_all(latitudinal, "mem", split_axis=1, concat_axis=0, tiled=True)
    arranged = gathered.reshape(gathered.shape[0], gathered.shape[1], shells, 3, 2)
    trig = fourier_table(order_map, vorticity.shape[3])
    velocity = jnp.einsum("mtsck,mkp->tscp", arranged, trig, preferred_element_type=F32)
    return cross_product(velocity, vorticity)


def synth_body(
    groups, members, spec_hbm, inv_hbm, leg_ref, deg_ref, ord_ref, send_ref,
    spec, inv, t0, t1, t2, i0, i1, i2, i3, solved, f0, f1, f2, sems,
):
    orders, radii, width = spec.shape[2:]
    shells = inv.shape[0]
    lats = leg_ref.shape[1]
    half = LANES // 2
    fill = 2 * LANES - radii
    rows = 3 * orders
    mine = shells // groups
    per_tile = LANES // orders

    inv_copy = pltpu.make_async_copy(inv_hbm, inv, sems.at[3])
    inv_copy.start()
    copies = [pltpu.make_async_copy(spec_hbm.at[c], spec.at[c], sems.at[c]) for c in range(3)]
    for copy in copies:
        copy.start()

    eye = (
        lax.broadcasted_iota(jnp.int32, (width, width), 0)
        == lax.broadcasted_iota(jnp.int32, (width, width), 1)
    ).astype(BF16)
    gap = jnp.zeros((fill, width), BF16)

    inv_copy.wait()

    def turn_inverse(s, carry):
        a = inv[s]
        out = nt(eye, jnp.concatenate([a, gap, gap, a], axis=0))
        at = pl.ds(pl.multiple_of(s * width, width), width)
        i0[at, :] = out[:, 0:LANES]
        i1[at, :] = out[:, LANES : 2 * LANES]
        i2[at, :] = out[:, 2 * LANES : 3 * LANES]
        i3[at, :] = out[:, 3 * LANES : 4 * LANES]
        return carry

    lax.fori_loop(0, shells, turn_inverse, 0, unroll=4)

    for c in range(3):
        copies[c].wait()

        def turn_profiles(m, carry):
            out = nt(eye, jnp.concatenate([spec[c, 0, m], spec[c, 1, m]], axis=0))
            at = pl.ds(pl.multiple_of((c * orders + m) * width, width), width)
            t0[at, :] = out[:, 0:LANES]
            t1[at, :] = out[:, LANES : 2 * LANES]
            t2[at, :] = out[:, 2 * LANES : 3 * LANES]
            return carry

        lax.fori_loop(0, orders, turn_profiles, 0, unroll=4)

    nothing = jnp.zeros((shells, LANES), BF16)
    pad = jnp.zeros((half - shells, 3 * LANES), BF16)

    def solve(l, carry):
        at = pl.ds(l, rows, stride=width)
        profiles = jnp.concatenate([r[at, :].astype(BF16) for r in (t0, t1, t2)], axis=1)
        on = pl.ds(l, shells, stride=width)
        real = jnp.concatenate([i0[on, :].astype(BF16), i1[on, :].astype(BF16), nothing], axis=1)
        imag = jnp.concatenate([nothing, i2[on, :].astype(BF16), i3[on, :].astype(BF16)], axis=1)
        solved[at, :] = nt(profiles, jnp.concatenate([real, pad, imag, pad], axis=0))
        return carry

    lax.fori_loop(0, width, solve, 0, unroll=4)

    degrees = deg_ref[...]

    def sum_degrees(m, carry):
        table = jnp.where(degrees >= ord_ref[m], leg_ref[m].astype(F32), 0.0).astype(BF16)
        block = jnp.concatenate(
            [
                solved[pl.ds(pl.multiple_of((c * orders + m) * width, width), width), :].astype(BF16)
                for c in range(3)
            ],
            axis=1,
        )
        out = nn(table, block)
        at = pl.ds(m, lats, stride=orders)
        f0[at, :] = out[:, 0:LANES]
        f1[at, :] = out[:, LANES : 2 * LANES]
        f2[at, :] = out[:, 2 * LANES : 3 * LANES]
        return carry

    lax.fori_loop(0, orders, sum_degrees, 0, unroll=4)

    row = lax.broadcasted_iota(jnp.int32, (2 * shells, LANES), 0)
    lane = lax.broadcasted_iota(jnp.int32, (2 * shells, LANES), 1)
    want = row
    for i in range(1, 2 * groups):
        g, k = i // 2, i % 2
        step = (half + g * mine - i * mine) if k else (g * mine - i * mine)
        want = jnp.where(row >= i * mine, row + step, want)
    pick = (want == lane).astype(BF16)
    tiles = lats // members // per_tile

    def turn_sums(j, carry):
        parts = []
        for b in range(tiles):
            at = pl.ds(pl.multiple_of((j * tiles + b) * LANES, LANES), LANES)
            parts += [nt(pick, f[at, :].astype(BF16)) for f in (f0, f1, f2)]
        for g in range(groups):
            block = [p[g * 2 * mine : (g + 1) * 2 * mine] for p in parts]
            send_ref[j, g] = jnp.concatenate(block, axis=0).astype(BF16)
        return carry

    lax.fori_loop(0, members, turn_sums, 0)


def synthesize(spec, inv, legendre, degrees, orders_here, groups, members):
    _, _, orders, radii, width = spec.shape
    shells = inv.shape[0]
    lats = legendre.shape[1]
    mine = shells // groups
    block = lats // members * orders * mine * 6 // LANES
    any_space = pl.BlockSpec(memory_space=pl.ANY)
    vmem = pl.BlockSpec(memory_space=pltpu.VMEM)
    return pl.pallas_call(
        functools.partial(synth_body, groups, members),
        out_shape=jax.ShapeDtypeStruct((members, groups, block, LANES), BF16),
        in_specs=[any_space, any_space, vmem, vmem, pl.BlockSpec(memory_space=pltpu.SMEM)],
        out_specs=vmem,
        scratch_shapes=[
            pltpu.VMEM(spec.shape, BF16),
            pltpu.VMEM(inv.shape, BF16),
            *[pltpu.VMEM((3 * orders * width, LANES), F32)] * 3,
            *[pltpu.VMEM((shells * width, LANES), F32)] * 4,
            pltpu.VMEM((3 * orders * width, LANES), F32),
            *[pltpu.VMEM((lats * orders, LANES), F32)] * 3,
            pltpu.SemaphoreType.DMA((4,)),
        ],
        compiler_params=pltpu.CompilerParams(vmem_limit_bytes=60 * 2**20),
        name="partial_sums",
    )(spec, inv, legendre, degrees, orders_here)


def physical_body(
    orders, recv_ref, vort_ref, near_ref, far_ref, out_ref, *keep
):
    members, block, _ = recv_ref.shape
    shells = vort_ref.shape[1]
    lats = vort_ref.shape[2]
    points = vort_ref.shape[3]
    per_tile = LANES // orders
    tiles = lats // per_tile
    for i in range(per_tile):
        for h in range(members // per_tile):
            parts = [
                recv_ref[h * per_tile + j].astype(F32)[:, i * orders : (i + 1) * orders]
                for j in range(per_tile)
            ]
            joined = jnp.concatenate(parts, axis=1)
            for b in range(tiles):
                for c in range(3):
                    for k in range(2):
                        at = ((b * 3 + c) * 2 + k) * shells
                        to = pl.ds(c * shells * lats + b * per_tile + i, shells, stride=lats)
                        keep[k * (members // per_tile) + h][to, :] = joined[at : at + shells]
    left = jnp.concatenate([r[...].astype(BF16) for r in keep], axis=1)
    flat = shells * lats
    for q in range(points // LANES):
        on = slice(q * LANES, (q + 1) * LANES)
        fc, fs = far_ref[0, :, q : q + 1], far_ref[1, :, q : q + 1]
        nc, ns = near_ref[0], near_ref[1]
        trig = jnp.concatenate([nc * fc - ns * fs, -(ns * fc + nc * fs)], axis=0).astype(BF16)
        v = nn(left, trig)
        v0, v1, v2 = v[:flat], v[flat : 2 * flat], v[2 * flat :]
        w0, w1, w2 = [vort_ref[c, :, :, on].reshape(flat, LANES).astype(F32) for c in range(3)]
        shape = (shells, lats, LANES)
        out_ref[0, :, :, on] = (v1 * w2 - v2 * w1).astype(BF16).reshape(shape)
        out_ref[1, :, :, on] = (v2 * w0 - v0 * w2).astype(BF16).reshape(shape)
        out_ref[2, :, :, on] = (v0 * w1 - v1 * w0).astype(BF16).reshape(shape)


def physical(received, vorticity, near, far, orders):
    members = received.shape[0]
    _, shells, lats, _ = vorticity.shape
    vmem = pl.BlockSpec(memory_space=pltpu.VMEM)
    return pl.pallas_call(
        functools.partial(physical_body, orders),
        out_shape=jax.ShapeDtypeStruct(vorticity.shape, BF16),
        in_specs=[vmem] * 4,
        out_specs=vmem,
        scratch_shapes=[pltpu.VMEM((3 * shells * lats, LANES), F32)]
        * (2 * members * orders // LANES),
        compiler_params=pltpu.CompilerParams(vmem_limit_bytes=40 * 2**20),
        name="physical",
    )(received, vorticity, near, far)


def trig_tables(order_map, count):
    def angle(p):
        phase = order_map[:, None] * p[None, :] % count
        return phase.astype(F32) * (2.0 * math.pi / count)

    weight = jnp.where(order_map == 0, 1.0, 2.0).astype(F32)[:, None]
    near = angle(jnp.arange(LANES, dtype=jnp.int32))
    far = angle(jnp.arange(LANES, dtype=jnp.int32) * LANES)
    return (
        jnp.stack([weight * jnp.cos(near), weight * jnp.sin(near)]),
        jnp.stack([jnp.cos(far), jnp.sin(far)]),
    )


def shards(groups, members, spectral, inverse, legendre, vorticity, degree_list, order_map):
    width = spectral.shape[0]
    orders = spectral.shape[3]
    spec = jnp.transpose(spectral, (1, 2, 3, 4, 0))
    inv = jnp.transpose(inverse, (1, 2, 0))
    vort = jnp.transpose(vorticity, (0, 2, 1, 3))
    degrees = lax.dynamic_slice_in_dim(degree_list, lax.axis_index("grp") * width, width)
    orders_here = lax.dynamic_slice_in_dim(order_map, lax.axis_index("mem") * orders, orders)
    near, far = trig_tables(order_map, vorticity.shape[3])
    partial = synthesize(
        spec, inv, legendre, degrees.reshape(1, width), orders_here, groups, members
    )
    summed = lax.psum_scatter(partial, "grp", scatter_dimension=1, tiled=False)
    received = lax.all_to_all(summed, "mem", split_axis=0, concat_axis=0, tiled=True)
    out = physical(received, vort, near, far, orders)
    return jnp.transpose(out, (0, 2, 1, 3))


def solution(mesh):
    groups, members = mesh.shape["grp"], mesh.shape["mem"]

    def local(spectral, inverse, legendre, vorticity, degree_list, order_map):
        args = (spectral, inverse, legendre, vorticity, degree_list, order_map)
        width, _, _, orders, radii = spectral.shape
        shells, lats = inverse.shape[1], legendre.shape[1]
        fits = (
            width == LANES
            and 2 * shells <= LANES
            and LANES < radii
            and 2 * radii == 3 * LANES
            and LANES % orders == 0
            and (shells // groups * 2) % 8 == 0
            and members % (LANES // orders) == 0
            and (lats // members) % (LANES // orders) == 0
            and vorticity.shape[3] % LANES == 0
            and vorticity.shape[3] // LANES <= LANES
        )
        if fits:
            return shards(groups, members, *args)
        return plain_shards(*args)

    return jax.shard_map(
        local,
        mesh=mesh,
        in_specs=(
            P("grp", None, None, "mem", None),
            P("grp", None, None),
            P("mem", None, "grp"),
            P(None, "mem", "grp", None),
            P(),
            P(),
        ),
        out_specs=P(None, "mem", "grp", None),
        check_vma=False,
    )
```

time: 121 us -> 116 us (0.959)
  Pallas kernels: 0 us -> 54.4 us
  local copies, waits for them, and re-layouts: 37.8 us -> 4.36 us
  matrix products: 13.6 us -> 0 us
  other arithmetic: 9.91 us -> 1.18 us
  starting transfers between devices: 11.1 us -> 5.49 us
  waiting for transfers between devices: 34.3 us -> 37 us
    pallas_call x0 -> x2, Pallas kernels: none -> 54.4 us  [the longest x1 51.6 us: synthesize(): pl.pallas_call(functools.partial(synth_body, groups, members), out_shape=...]
    reduce_scatter x0 -> x1, waiting for transfers between devices: none -> 28.6 us  [shards(): summed = lax.psum_scatter(partial, 'grp', scatter_dimension=1, tiled=False)]
    all_to_all x2 -> x1, waiting for transfers between devices: 33.6 us -> 8.42 us  [shards(): lax.all_to_all(summed, 'mem', split_axis=0, concat_axis=0, tiled=True)]
    reshape x3 -> x1, local copies, waits for them, and re-layouts: 22.4 us -> 0.58 us  [shards(): degrees.reshape(1, width)]
    dot_general x3 -> x0, matrix products: 13.6 us -> none  [the longest x1 9.62 us: solve_radial(): lax.dot_general(rows, flat_profiles, (((2,), (2,)), ((0,), (0,))), prefer...]
    another operation x3 -> x1, other arithmetic: 8.02 us -> 0.04 us  [trig_tables(): jnp.stack([weight * jnp.cos(near), weight * jnp.sin(near)])]
    all_to_all x2 -> x1, starting transfers between devices: 11.1 us -> 5.49 us  [shards(): lax.all_to_all(summed, 'mem', split_axis=0, concat_axis=0, tiled=True)]
    all_to_all x2 -> x0, local copies, waits for them, and re-layouts: 5.02 us -> none  [the longest x1 3.24 us: shards(): lax.all_to_all(radial_factor, 'grp', split_axis=1, concat_axis=0, tiled=T...]
  transfers between devices with their start and end apart: 3 -> 2, of which waited for: 2 -> 2; matrix products, arithmetic and copies ran while one was open for 42% -> 1% of each run, Pallas kernels for 0% -> 0%
where the time goes in v1:
time: 116 us
  Pallas kernels  54.4 us (47%)
  waiting for transfers between devices  37 us (32%)
  between operations  13.5 us (12%)
  starting transfers between devices  5.49 us (5%)
  local copies, waits for them, and re-layouts  4.36 us (4%)
  other arithmetic  1.18 us (1%)
    pallas_call x1, Pallas kernels, synthesize(): pl.pallas_call(functools.partial(synth_body, groups, members), out_shape=...  51.6 us
    reduce_scatter x1, waiting for transfers between devices, shards(): summed = lax.psum_scatter(partial, 'grp', scatter_dimension=1, tiled=False)  28.6 us
    all_to_all x1, waiting for transfers between devices, shards(): lax.all_to_all(summed, 'mem', split_axis=0, concat_axis=0, tiled=True)  8.42 us
    all_to_all x1, starting transfers between devices, shards(): lax.all_to_all(summed, 'mem', split_axis=0, concat_axis=0, tiled=True)  5.49 us
    pallas_call x1, Pallas kernels, physical(): pl.pallas_call(functools.partial(physical_body, orders), out_shape=jax.Sh...  2.78 us
    pallas_call x1, local copies, waits for them, and re-layouts, synthesize(): pl.pallas_call(functools.partial(synth_body, groups, members), out_shape=...  2.45 us
  transfers between devices with their start and end apart: 2, of which 2 were waited for; matrix products, arithmetic and copies ran while one was open for 1% of the time, Pallas kernels for 0%

profile of v1, /device:TPU:0, one launch (start us, length us, event | category | flops | bytes accessed | tf_op | source)
XLA Modules:
  0.0 115.9 jit_solution(9548995007215092561)
XLA Ops:
  6.5 0.0 copy-start
  6.5 0.0 reduce-scatter.2.cloned.1.call-start
  6.5 1.3 %dynamic_slice.7.ord_ref = s32[32]{0:T(128)} dynamic-slice(s32[256]{0:T(256)} %param.11, s32[]{:T(128)S(6)} %select_n.44), dynamic_slice_sizes={32} | dynamic-slice | bytes 260 | tf_op jit(solution)/shard_map/dynamic_slice | solution.py:283
  7.8 0.0 copy-done
  7.8 0.6 dynamic-slice_bitcast_fusion.deg_ref
  8.4 51.6 %partial_sums.1 = bf16[8,4,144,128]{3,2,1,0:T(8,128)(2,1)} custom-call(bf16[3,2,32,192,128]{4,3,2,1,0:T(8,128)(2,1)} %bitcast.8, bf16[48,192,128]{2,1,0:T(8,128)(2,1)} %bitcast.9, bf16[32,64,128]{2,1,0:T(8,128)(2,1)} %leg_ref.1, s32[1,128]{1,0:T(1,128)} %dynamic-slice_bitcast_fusion.deg_ref, s32[32]{0:T(128)} %dynamic_slice.7.ord_ref), custom_call_target="tpu_custom_call" | custom-call | tf_op jit(solution)/shard_map/partial_sums/pallas_call | solution.py:189
  60.0 0.0 copy-start.2
  60.1 0.0 copy-start.1
  60.1 2.5 %copy.7 = bf16[8,4,144,128]{3,2,0,1:T(8,128)(2,1)} copy(bf16[8,4,144,128]{3,2,1,0:T(8,128)(2,1)} %partial_sums.1) | data formatting | bytes 2359296 | tf_op jit(solution)/shard_map/partial_sums/pallas_call | solution.py:189
  62.5 0.0 reduce-scatter.2.cloned.1.call-update
  62.5 28.6 %reduce-scatter.2.cloned.1.call-done = bf16[8,1,144,128]{3,2,0,1:T(8,128)(2,1)} async-done(((bf16[8,4,144,128]{3,2,0,1:T(8,128)(2,1)}), bf16[8,1,144,128]{3,2,0,1:T(8,128)(2,1)}) %reduce-scatter.2.cloned.1.call-update) | async-done | bytes 294928 | tf_op jit(solution)/shard_map/reduce_scatter | solution.py:288
  91.1 5.5 %all-to-all-start = ((bf16[8,144,128]{2,1,0:T(8,128)(2,1)}), bf16[8,144,128]{2,1,0:T(8,128)(2,1)S(1)}, u32[]{:S(2)}, u32[]{:S(2)}) async-start(bf16[8,144,128]{2,1,0:T(8,128)(2,1)} %bitcast.10), calls=%async_computation.1 | async-start | bytes 589824 | tf_op jit(solution)/shard_map/all_to_all | solution.py:289
  96.6 0.0 copy-done.2
  96.7 1.1 fusion.7
  97.8 8.4 %all-to-all-done.recv_ref = bf16[8,144,128]{2,1,0:T(8,128)(2,1)S(1)} async-done(((bf16[8,144,128]{2,1,0:T(8,128)(2,1)}), bf16[8,144,128]{2,1,0:T(8,128)(2,1)S(1)}, u32[]{:S(2)}, u32[]{:S(2)}) %all-to-all-start) | async-done | bytes 294944 | tf_op jit(solution)/shard_map/all_to_all | solution.py:289
  106.3 0.0 copy-done.1
  106.3 2.8 %physical.1 = bf16[3,12,8,1536]{3,2,1,0:T(8,128)(2,1)} custom-call(bf16[8,144,128]{2,1,0:T(8,128)(2,1)S(1)} %all-to-all-done.recv_ref, bf16[3,12,8,1536]{3,2,1,0:T(8,128)(2,1)S(1)} %bitcast.7, f32[2,256,128]{2,1,0:T(8,128)S(1)} %get-tuple-element.11.near_ref, f32[2,256,128]{2,1,0:T(8,128)S(1)} %get-tuple-element.12.far_ref), custom_call_target="tpu_custom_call" | custom-call | tf_op jit(solution)/shard_map/physical/pallas_call | solution.py:250
  (3 shorter events, 0.0 us)
Async XLA Ops:
  6.5 1.3 %copy-start = (s32[512]{0:T(512)S(1)}, s32[512]{0:T(512)}, u32[]{:S(2)}) copy-start(s32[512]{0:T(512)} %param.10) | copy-start | bytes 6148
  6.5 84.6 %reduce-scatter.2.cloned.1.call-start = ((), (), s32[]{:S(2)}) async-start(), calls=%async_computation.2 | async-start | bytes 1474560 | tf_op jit(solution)/shard_map/reduce_scatter | solution.py:288
  60.0 36.6 %copy-start.2 = (s32[256]{0:T(256)S(1)}, s32[256]{0:T(256)}, u32[]{:S(2)}) copy-start(s32[256]{0:T(256)} %param.11) | copy-start | bytes 3076
  60.1 46.2 %copy-start.1 = (bf16[3,8,12,1536]{3,1,2,0:T(8,128)(2,1)S(1)}, bf16[3,8,12,1536]{3,1,2,0:T(8,128)(2,1)}, u32[]{:S(2)}) copy-start(bf16[3,8,12,1536]{3,1,2,0:T(8,128)(2,1)} %param.9) | copy-start | bytes 2654212
  91.1 15.1 %all-to-all-start = ((bf16[8,144,128]{2,1,0:T(8,128)(2,1)}), bf16[8,144,128]{2,1,0:T(8,128)(2,1)S(1)}, u32[]{:S(2)}, u32[]{:S(2)}) async-start(bf16[8,144,128]{2,1,0:T(8,128)(2,1)} %bitcast.10), calls=%async_computation.1 | async-start | bytes 589824 | tf_op jit(solution)/shard_map/all_to_all | solution.py:289
Sparse Core Ops, SparseCore 0:
  62.7 28.4 reduce-scatter.1

commit v2 on v1

--- a/solution.py
+++ b/solution.py
@@ -81,6 +81,7 @@
     rows = 3 * orders
     mine = shells // groups
     per_tile = LANES // orders
+    pitch, lat_pitch = width + 1, orders + 1
 
     inv_copy = pltpu.make_async_copy(inv_hbm, inv, sems.at[3])
     inv_copy.start()
@@ -99,7 +100,7 @@
     def turn_inverse(s, carry):
         a = inv[s]
         out = nt(eye, jnp.concatenate([a, gap, gap, a], axis=0))
-        at = pl.ds(pl.multiple_of(s * width, width), width)
+        at = pl.ds(s * pitch, width)
         i0[at, :] = out[:, 0:LANES]
         i1[at, :] = out[:, LANES : 2 * LANES]
         i2[at, :] = out[:, 2 * LANES : 3 * LANES]
@@ -113,7 +114,7 @@
 
         def turn_profiles(m, carry):
             out = nt(eye, jnp.concatenate([spec[c, 0, m], spec[c, 1, m]], axis=0))
-            at = pl.ds(pl.multiple_of((c * orders + m) * width, width), width)
+            at = pl.ds((c * orders + m) * pitch, width)
             t0[at, :] = out[:, 0:LANES]
             t1[at, :] = out[:, LANES : 2 * LANES]
             t2[at, :] = out[:, 2 * LANES : 3 * LANES]
@@ -125,9 +126,9 @@
     pad = jnp.zeros((half - shells, 3 * LANES), BF16)
 
     def solve(l, carry):
-        at = pl.ds(l, rows, stride=width)
+        at = pl.ds(l, rows, stride=pitch)
         profiles = jnp.concatenate([r[at, :].astype(BF16) for r in (t0, t1, t2)], axis=1)
-        on = pl.ds(l, shells, stride=width)
+        on = pl.ds(l, shells, stride=pitch)
         real = jnp.concatenate([i0[on, :].astype(BF16), i1[on, :].astype(BF16), nothing], axis=1)
         imag = jnp.concatenate([nothing, i2[on, :].astype(BF16), i3[on, :].astype(BF16)], axis=1)
         solved[at, :] = nt(profiles, jnp.concatenate([real, pad, imag, pad], axis=0))
@@ -141,13 +142,13 @@
         table = jnp.where(degrees >= ord_ref[m], leg_ref[m].astype(F32), 0.0).astype(BF16)
         block = jnp.concatenate(
             [
-                solved[pl.ds(pl.multiple_of((c * orders + m) * width, width), width), :].astype(BF16)
+                solved[pl.ds((c * orders + m) * pitch, width), :].astype(BF16)
                 for c in range(3)
             ],
             axis=1,
         )
         out = nn(table, block)
-        at = pl.ds(m, lats, stride=orders)
+        at = pl.ds(m, lats, stride=lat_pitch)
         f0[at, :] = out[:, 0:LANES]
         f1[at, :] = out[:, LANES : 2 * LANES]
         f2[at, :] = out[:, 2 * LANES : 3 * LANES]
@@ -168,11 +169,16 @@
     def turn_sums(j, carry):
         parts = []
         for b in range(tiles):
-            at = pl.ds(pl.multiple_of((j * tiles + b) * LANES, LANES), LANES)
-            parts += [nt(pick, f[at, :].astype(BF16)) for f in (f0, f1, f2)]
+            at = [
+                pl.ds(((j * tiles + b) * per_tile + i) * lat_pitch, orders)
+                for i in range(per_tile)
+            ]
+            for f in (f0, f1, f2):
+                both = jnp.concatenate([f[a, :].astype(BF16) for a in at], axis=0)
+                parts.append(nt(pick, both))
         for g in range(groups):
             block = [p[g * 2 * mine : (g + 1) * 2 * mine] for p in parts]
-            send_ref[j, g] = jnp.concatenate(block, axis=0).astype(BF16)
+            send_ref[j, g % 2, g // 2] = jnp.concatenate(block, axis=0).astype(BF16)
         return carry
 
     lax.fori_loop(0, members, turn_sums, 0)
@@ -184,25 +190,147 @@
     lats = legendre.shape[1]
     mine = shells // groups
     block = lats // members * orders * mine * 6 // LANES
+    pitch = width + 1
     any_space = pl.BlockSpec(memory_space=pl.ANY)
     vmem = pl.BlockSpec(memory_space=pltpu.VMEM)
     return pl.pallas_call(
         functools.partial(synth_body, groups, members),
-        out_shape=jax.ShapeDtypeStruct((members, groups, block, LANES), BF16),
+        out_shape=jax.ShapeDtypeStruct((members, 2, groups // 2, block, LANES), BF16),
         in_specs=[any_space, any_space, vmem, vmem, pl.BlockSpec(memory_space=pltpu.SMEM)],
         out_specs=vmem,
         scratch_shapes=[
             pltpu.VMEM(spec.shape, BF16),
             pltpu.VMEM(inv.shape, BF16),
-            *[pltpu.VMEM((3 * orders * width, LANES), F32)] * 3,
-            *[pltpu.VMEM((shells * width, LANES), F32)] * 4,
-            pltpu.VMEM((3 * orders * width, LANES), F32),
-            *[pltpu.VMEM((lats * orders, LANES), F32)] * 3,
+            *[pltpu.VMEM((3 * orders * pitch, LANES), F32)] * 3,
+            *[pltpu.VMEM((shells * pitch, LANES), F32)] * 4,
+            pltpu.VMEM((3 * orders * pitch, LANES), F32),
+            *[pltpu.VMEM((lats * (orders + 1), LANES), F32)] * 3,
             pltpu.SemaphoreType.DMA((4,)),
         ],
         compiler_params=pltpu.CompilerParams(vmem_limit_bytes=60 * 2**20),
         name="partial_sums",
     )(spec, inv, legendre, degrees, orders_here)
+
+
+MESH = pl.DeviceIdType.MESH
+
+
+def exchange_body(
+    send_ref, out_ref, from_sib, to_far, from_far, to_mem, recv,
+    sib_s, sib_r, far_s, far_r, mem_s, mem_r,
+):
+    members = send_ref.shape[0]
+    grp, me = lax.axis_index("grp"), lax.axis_index("mem")
+    y, core = grp // 2, grp % 2
+    sibling = y * 2 + (1 - core)
+    across = (1 - y) * 2 + core
+
+    barrier = pltpu.get_barrier_semaphore()
+    for g in (sibling, across):
+        pl.semaphore_signal(barrier, inc=1, device_id=(g, me), device_id_type=MESH)
+    for i in range(1, members):
+        pl.semaphore_signal(
+            barrier, inc=1, device_id=(grp, (me + i) % members), device_id_type=MESH
+        )
+    pl.semaphore_wait(barrier, members + 1)
+
+    def to_sibling(j):
+        return pltpu.make_async_remote_copy(
+            src_ref=send_ref.at[j, 1 - core], dst_ref=from_sib.at[j],
+            send_sem=sib_s.at[j], recv_sem=sib_r.at[j],
+            device_id=(sibling, me), device_id_type=MESH,
+        )
+
+    def to_across(j):
+        return pltpu.make_async_remote_copy(
+            src_ref=to_far.at[j], dst_ref=from_far.at[j],
+            send_sem=far_s.at[j], recv_sem=far_r.at[j],
+            device_id=(across, me), device_id_type=MESH,
+        )
+
+    def to_member(j, slot):
+        return pltpu.make_async_remote_copy(
+            src_ref=to_mem.at[j], dst_ref=recv.at[slot],
+            send_sem=mem_s.at[j], recv_sem=mem_r.at[slot],
+            device_id=(grp, j), device_id_type=MESH,
+        )
+
+    def target(i):
+        return (me + 1 + i) % members
+
+    def start(i, carry):
+        to_sibling(target(i)).start()
+        return carry
+
+    lax.fori_loop(0, members, start, 0)
+
+    def pair_sum(j, half):
+        return send_ref[j, core, half].astype(F32) + from_sib[j, half].astype(F32)
+
+    def second(i, carry):
+        j = target(i)
+        to_sibling(j).wait_recv()
+        to_far[j] = pair_sum(j, 1 - y).astype(BF16)
+        to_across(j).start()
+        return carry
+
+    lax.fori_loop(0, members, second, 0)
+
+    def total(j):
+        to_across(j).wait_recv()
+        return (pair_sum(j, y) + from_far[j].astype(F32)).astype(BF16)
+
+    def third(i, carry):
+        j = target(i)
+        to_mem[j] = total(j)
+        to_member(j, me).start()
+        return carry
+
+    lax.fori_loop(0, members - 1, third, 0)
+    out_ref[me] = total(me)
+
+    def finish(i, carry):
+        j = target(i)
+        to_member(j, j).wait_recv()
+        out_ref[j] = recv[j]
+        return carry
+
+    lax.fori_loop(0, members - 1, finish, 0)
+
+    def drain(i, carry):
+        j = target(i)
+        to_sibling(j).wait_send()
+        to_across(j).wait_send()
+        return carry
+
+    lax.fori_loop(0, members, drain, 0)
+
+    def drain_members(i, carry):
+        to_member(target(i), me).wait_send()
+        return carry
+
+    lax.fori_loop(0, members - 1, drain_members, 0)
+
+
+def exchange(partial):
+    members, cores, far, block, _ = partial.shape
+    vmem = pl.BlockSpec(memory_space=pltpu.VMEM)
+    slots = pltpu.VMEM((members, block, LANES), BF16)
+    return pl.pallas_call(
+        exchange_body,
+        out_shape=jax.ShapeDtypeStruct((members, block, LANES), BF16),
+        in_specs=[vmem],
+        out_specs=vmem,
+        scratch_shapes=[
+            pltpu.VMEM((members, far, block, LANES), BF16),
+            slots, slots, slots, slots,
+            *[pltpu.SemaphoreType.DMA((members,))] * 6,
+        ],
+        compiler_params=pltpu.CompilerParams(
+            collective_id=0, has_side_effects=True, vmem_limit_bytes=32 * 2**20
+        ),
+        name="exchange",
+    )(partial)
 
 
 def physical_body(
@@ -285,8 +413,7 @@
     partial = synthesize(
         spec, inv, legendre, degrees.reshape(1, width), orders_here, groups, members
     )
-    summed = lax.psum_scatter(partial, "grp", scatter_dimension=1, tiled=False)
-    received = lax.all_to_all(summed, "mem", split_axis=0, concat_axis=0, tiled=True)
+    received = exchange(partial)
     out = physical(received, vort, near, far, orders)
     return jnp.transpose(out, (0, 2, 1, 3))
 
@@ -299,7 +426,8 @@
         width, _, _, orders, radii = spectral.shape
         shells, lats = inverse.shape[1], legendre.shape[1]
         fits = (
-            width == LANES
+            groups == 4
+            and width == LANES
             and 2 * shells <= LANES
             and LANES < radii
             and 2 * radii == 3 * LANES

time: 116 us -> 53.8 us (0.46)
  waiting for transfers between devices: 37 us -> 0 us
  between operations: 13.5 us -> 0.07 us
  starting transfers between devices: 5.49 us -> 0 us
  Pallas kernels: 54.4 us -> 49.2 us
  local copies, waits for them, and re-layouts: 4.36 us -> 3.12 us
    reduce_scatter x1 -> x0, waiting for transfers between devices: 28.6 us -> none  [shards(): summed = lax.psum_scatter(partial, 'grp', scatter_dimension=1, tiled=False)]
    pallas_call x1, Pallas kernels: 51.6 us -> 27.8 us  [synthesize(): pl.pallas_call(functools.partial(synth_body, groups, members), out_shape=...]
    pallas_call x0 -> x1, Pallas kernels: none -> 18.9 us  [exchange(): pl.pallas_call(exchange_body, out_shape=jax.ShapeDtypeStruct((members, bl...]
    all_to_all x1 -> x0, waiting for transfers between devices: 8.42 us -> none  [shards(): lax.all_to_all(summed, 'mem', split_axis=0, concat_axis=0, tiled=True)]
    all_to_all x1 -> x0, starting transfers between devices: 5.49 us -> none  [shards(): lax.all_to_all(summed, 'mem', split_axis=0, concat_axis=0, tiled=True)]
    pallas_call x1 -> x0, local copies, waits for them, and re-layouts: 2.45 us -> none  [synthesize(): pl.pallas_call(functools.partial(synth_body, groups, members), out_shape=...]
    unnamed x6 -> x8, local copies, waits for them, and re-layouts: 0.02 us -> 1.28 us
  transfers between devices with their start and end apart: 2 -> 0, of which waited for: 2 -> 0; matrix products, arithmetic and copies ran while one was open for 1% -> 0% of each run, Pallas kernels for 0% -> 0%
where the time goes in v2:
time: 53.8 us; the launch traced here: 53.6 us
  Pallas kernels  49.2 us (91%)
  local copies, waits for them, and re-layouts  3.12 us (6%)
  other arithmetic  1.18 us (2%)
    pallas_call x1, Pallas kernels, synthesize(): pl.pallas_call(functools.partial(synth_body, groups, members), out_shape=...  27.8 us
    pallas_call x1, Pallas kernels, exchange(): pl.pallas_call(exchange_body, out_shape=jax.ShapeDtypeStruct((members, bl...  18.9 us
    pallas_call x1, Pallas kernels, physical(): pl.pallas_call(functools.partial(physical_body, orders), out_shape=jax.Sh...  2.6 us
    unnamed x8, local copies, waits for them, and re-layouts  1.28 us
    dynamic_slice x1, local copies, waits for them, and re-layouts, shards(): lax.dynamic_slice_in_dim(order_map, lax.axis_index('mem') * orders, orders)  1.27 us
    cos x1, other arithmetic, trig_tables(): jnp.cos(far)  1.14 us

profile of v2, /device:TPU:0, one launch (start us, length us, event | category | flops | bytes accessed | tf_op | source)
XLA Modules:
  0.0 53.6 jit_solution(15856338171716339946)
XLA Ops:
  0.0 0.0 copy-start
  0.0 1.3 %dynamic_slice.7.ord_ref = s32[32]{0:T(128)} dynamic-slice(s32[256]{0:T(256)} %param.11, s32[]{:T(128)S(6)} %select_n.44), dynamic_slice_sizes={32} | dynamic-slice | bytes 260 | tf_op jit(solution)/shard_map/dynamic_slice | solution.py:411
  1.3 0.0 copy-done
  1.3 0.6 %dynamic-slice_bitcast_fusion.deg_ref = s32[1,128]{1,0:T(1,128)} fusion(s32[512]{0:T(512)S(1)} %copy-done, s32[]{:T(128)S(6)} %select_n.43), kind=kLoop, calls=%fused_computation.22 | loop fusion | bytes 1028 | tf_op jit(solution)/shard_map/reshape | solution.py:414
  1.9 0.0 copy-start.3
  1.9 27.8 %partial_sums.1.send_ref = bf16[8,2,2,144,128]{4,3,2,1,0:T(8,128)(2,1)} custom-call(bf16[3,2,32,192,128]{4,3,2,1,0:T(8,128)(2,1)} %bitcast.7, bf16[48,192,128]{2,1,0:T(8,128)(2,1)} %bitcast.8, bf16[32,64,128]{2,1,0:T(8,128)(2,1)} %leg_ref.1, s32[1,128]{1,0:T(1,128)} %dynamic-slice_bitcast_fusion.deg_ref, s32[32]{0:T(128)} %dynamic_slice.7.ord_ref), custom_call_target="tpu_custom_call" | custom-call | tf_op jit(solution)/shard_map/partial_sums/pallas_call | solution.py:196
  29.6 0.0 copy-start.1
  29.6 1.3 %copy-done.1 = bf16[8,2,2,144,128]{4,3,2,1,0:T(8,128)(2,1)S(1)} copy-done((bf16[8,2,2,144,128]{4,3,2,1,0:T(8,128)(2,1)S(1)}, bf16[8,2,2,144,128]{4,3,2,1,0:T(8,128)(2,1)}, u32[]{:S(2)}) %copy-start.1) | copy-done | bytes 1179672
  30.9 0.0 copy-start.2
  30.9 18.9 %exchange.1.recv_ref = bf16[8,144,128]{2,1,0:T(8,128)(2,1)S(1)} custom-call(bf16[8,2,2,144,128]{4,3,2,1,0:T(8,128)(2,1)S(1)} %copy-done.1), custom_call_target="tpu_custom_call" | custom-call | tf_op jit(solution)/shard_map/exchange/pallas_call | solution.py:319
  49.8 0.0 copy-done.3
  49.8 1.1 %fusion.7 = (f32[1,256,128]{2,1,0:T(8,128)S(1)}, f32[1,256,128]{2,1,0:T(8,128)S(1)}, f32[1,256,128]{2,1,0:T(8,128)S(1)}, f32[1,256,128]{2,1,0:T(8,128)S(1)}) fusion(s32[128]{0:T(128)S(1)} %iota_multiply_fusion, s32[256]{0:T(256)S(1)} %copy-done.3, f32[256]{0:T(256)S(1)} %compare_select_fusion), kind=kLoop, calls=%fused_computation.12 | loop fusion | flops 655360 | bytes 526848 | tf_op jit(solution)/shard_map/cos | solution.py:400
  51.0 0.0 copy-done.2
  51.0 2.6 %physical.1 = bf16[3,12,8,1536]{3,2,1,0:T(8,128)(2,1)} custom-call(bf16[8,144,128]{2,1,0:T(8,128)(2,1)S(1)} %exchange.1.recv_ref, bf16[3,12,8,1536]{3,2,1,0:T(8,128)(2,1)S(1)} %bitcast.6, f32[2,256,128]{2,1,0:T(8,128)S(1)} %get-tuple-element.11.near_ref, f32[2,256,128]{2,1,0:T(8,128)S(1)} %get-tuple-element.12.far_ref), custom_call_target="tpu_custom_call" | custom-call | tf_op jit(solution)/shard_map/physical/pallas_call | solution.py:378
  (3 shorter events, 0.0 us)
Async XLA Ops:
  0.0 1.3 %copy-start = (s32[512]{0:T(512)S(1)}, s32[512]{0:T(512)}, u32[]{:S(2)}) copy-start(s32[512]{0:T(512)} %param.10) | copy-start | bytes 6148
  1.9 47.9 %copy-start.3 = (s32[256]{0:T(256)S(1)}, s32[256]{0:T(256)}, u32[]{:S(2)}) copy-start(s32[256]{0:T(256)} %param.11) | copy-start | bytes 3076
  29.6 1.3 %copy-start.1 = (bf16[8,2,2,144,128]{4,3,2,1,0:T(8,128)(2,1)S(1)}, bf16[8,2,2,144,128]{4,3,2,1,0:T(8,128)(2,1)}, u32[]{:S(2)}) copy-start(bf16[8,2,2,144,128]{4,3,2,1,0:T(8,128)(2,1)} %partial_sums.1.send_ref) | copy-start | bytes 3538948
  30.9 20.1 %copy-start.2 = (bf16[3,8,12,1536]{3,1,2,0:T(8,128)(2,1)S(1)}, bf16[3,8,12,1536]{3,1,2,0:T(8,128)(2,1)}, u32[]{:S(2)}) copy-start(bf16[3,8,12,1536]{3,1,2,0:T(8,128)(2,1)} %param.9) | copy-start | bytes 2654212

commit v3 on v2

--- a/solution.py
+++ b/solution.py
@@ -71,13 +71,12 @@
 
 def synth_body(
     groups, members, spec_hbm, inv_hbm, leg_ref, deg_ref, ord_ref, send_ref,
-    spec, inv, t0, t1, t2, i0, i1, i2, i3, solved, f0, f1, f2, sems,
+    spec, inv, t0, t1, t2, main, rest, solved, f0, f1, f2, sems,
 ):
     orders, radii, width = spec.shape[2:]
     shells = inv.shape[0]
     lats = leg_ref.shape[1]
     half = LANES // 2
-    fill = 2 * LANES - radii
     rows = 3 * orders
     mine = shells // groups
     per_tile = LANES // orders
@@ -90,56 +89,68 @@
         copy.start()
 
     eye = (
-        lax.broadcasted_iota(jnp.int32, (width, width), 0)
-        == lax.broadcasted_iota(jnp.int32, (width, width), 1)
+        lax.broadcasted_iota(jnp.int32, (2 * width, 2 * width), 0)
+        == lax.broadcasted_iota(jnp.int32, (2 * width, 2 * width), 1)
     ).astype(BF16)
-    gap = jnp.zeros((fill, width), BF16)
 
     inv_copy.wait()
 
-    def turn_inverse(s, carry):
-        a = inv[s]
-        out = nt(eye, jnp.concatenate([a, gap, gap, a], axis=0))
-        at = pl.ds(s * pitch, width)
-        i0[at, :] = out[:, 0:LANES]
-        i1[at, :] = out[:, LANES : 2 * LANES]
-        i2[at, :] = out[:, 2 * LANES : 3 * LANES]
-        i3[at, :] = out[:, 3 * LANES : 4 * LANES]
-        return carry
-
-    lax.fori_loop(0, shells, turn_inverse, 0, unroll=4)
+    def turn_inverse(i, carry):
+        both = jnp.concatenate([inv[2 * i], inv[2 * i + 1]], axis=1)
+        out = nt(eye, jnp.concatenate([both, both[LANES:]], axis=0))
+        for h in range(2):
+            at = pl.ds((2 * i + h) * pitch, width)
+            part = out[h * width : (h + 1) * width]
+            main[at, :] = part[:, 0:LANES]
+            rest[at, :] = part[:, LANES : 2 * LANES]
+        return carry
+
+    lax.fori_loop(0, shells // 2, turn_inverse, 0, unroll=4)
 
     for c in range(3):
         copies[c].wait()
 
-        def turn_profiles(m, carry):
-            out = nt(eye, jnp.concatenate([spec[c, 0, m], spec[c, 1, m]], axis=0))
-            at = pl.ds((c * orders + m) * pitch, width)
-            t0[at, :] = out[:, 0:LANES]
-            t1[at, :] = out[:, LANES : 2 * LANES]
-            t2[at, :] = out[:, 2 * LANES : 3 * LANES]
+        def turn_profiles(i, carry):
+            a, b = [
+                jnp.concatenate([spec[c, k, 2 * i], spec[c, k, 2 * i + 1]], axis=1)
+                for k in range(2)
+            ]
+            out = nt(eye, jnp.concatenate([a, b[LANES:], b[:LANES]], axis=0))
+            for h in range(2):
+                at = pl.ds((c * orders + 2 * i + h) * pitch, width)
+                part = out[h * width : (h + 1) * width]
+                t0[at, :] = part[:, 0:LANES]
+                t1[at, :] = part[:, LANES : 2 * LANES]
+                t2[at, :] = part[:, 2 * LANES : 3 * LANES]
             return carry
 
-        lax.fori_loop(0, orders, turn_profiles, 0, unroll=4)
+        lax.fori_loop(0, orders // 2, turn_profiles, 0, unroll=4)
 
     nothing = jnp.zeros((shells, LANES), BF16)
     pad = jnp.zeros((half - shells, 3 * LANES), BF16)
+    low = lax.broadcasted_iota(jnp.int32, (shells, LANES), 1) < half
 
     def solve(l, carry):
         at = pl.ds(l, rows, stride=pitch)
         profiles = jnp.concatenate([r[at, :].astype(BF16) for r in (t0, t1, t2)], axis=1)
         on = pl.ds(l, shells, stride=pitch)
-        real = jnp.concatenate([i0[on, :].astype(BF16), i1[on, :].astype(BF16), nothing], axis=1)
-        imag = jnp.concatenate([nothing, i2[on, :].astype(BF16), i3[on, :].astype(BF16)], axis=1)
+        first, last = main[on, :].astype(BF16), rest[on, :]
+        lower = jnp.where(low, last, 0.0).astype(BF16)
+        upper = jnp.where(low, 0.0, last).astype(BF16)
+        real = jnp.concatenate([first, lower, nothing], axis=1)
+        imag = jnp.concatenate([nothing, upper, first], axis=1)
         solved[at, :] = nt(profiles, jnp.concatenate([real, pad, imag, pad], axis=0))
         return carry
 
-    lax.fori_loop(0, width, solve, 0, unroll=4)
-
-    degrees = deg_ref[...]
+    lax.fori_loop(0, width, solve, 0, unroll=16)
+
+    start = pl.multiple_of(lax.axis_index("grp") * width, width)
+    degrees = deg_ref[pl.ds(start, width)].reshape(1, width)
+    first_order = lax.axis_index("mem") * orders
 
     def sum_degrees(m, carry):
-        table = jnp.where(degrees >= ord_ref[m], leg_ref[m].astype(F32), 0.0).astype(BF16)
+        valid = degrees >= ord_ref[first_order + m]
+        table = jnp.where(valid, leg_ref[m].astype(F32), 0.0).astype(BF16)
         block = jnp.concatenate(
             [
                 solved[pl.ds((c * orders + m) * pitch, width), :].astype(BF16)
@@ -154,7 +165,7 @@
         f2[at, :] = out[:, 2 * LANES : 3 * LANES]
         return carry
 
-    lax.fori_loop(0, orders, sum_degrees, 0, unroll=4)
+    lax.fori_loop(0, orders, sum_degrees, 0, unroll=8)
 
     row = lax.broadcasted_iota(jnp.int32, (2 * shells, LANES), 0)
     lane = lax.broadcasted_iota(jnp.int32, (2 * shells, LANES), 1)
@@ -181,10 +192,10 @@
             send_ref[j, g % 2, g // 2] = jnp.concatenate(block, axis=0).astype(BF16)
         return carry
 
-    lax.fori_loop(0, members, turn_sums, 0)
-
-
-def synthesize(spec, inv, legendre, degrees, orders_here, groups, members):
+    lax.fori_loop(0, members, turn_sums, 0, unroll=2)
+
+
+def synthesize(spec, inv, legendre, degree_list, order_map, groups, members):
     _, _, orders, radii, width = spec.shape
     shells = inv.shape[0]
     lats = legendre.shape[1]
@@ -202,14 +213,14 @@
             pltpu.VMEM(spec.shape, BF16),
             pltpu.VMEM(inv.shape, BF16),
             *[pltpu.VMEM((3 * orders * pitch, LANES), F32)] * 3,
-            *[pltpu.VMEM((shells * pitch, LANES), F32)] * 4,
+            *[pltpu.VMEM((shells * pitch, LANES), F32)] * 2,
             pltpu.VMEM((3 * orders * pitch, LANES), F32),
             *[pltpu.VMEM((lats * (orders + 1), LANES), F32)] * 3,
             pltpu.SemaphoreType.DMA((4,)),
         ],
         compiler_params=pltpu.CompilerParams(vmem_limit_bytes=60 * 2**20),
         name="partial_sums",
-    )(spec, inv, legendre, degrees, orders_here)
+    )(spec, inv, legendre, degree_list, order_map)
 
 
 MESH = pl.DeviceIdType.MESH
@@ -334,8 +345,10 @@
 
 
 def physical_body(
-    orders, recv_ref, vort_ref, near_ref, far_ref, out_ref, *keep
+    orders, recv_ref, vort_hbm, near_ref, far_ref, out_ref, vort_ref, sem, *keep
 ):
+    copy = pltpu.make_async_copy(vort_hbm, vort_ref, sem.at[0])
+    copy.start()
     members, block, _ = recv_ref.shape
     shells = vort_ref.shape[1]
     lats = vort_ref.shape[2]
@@ -357,6 +370,7 @@
                         keep[k * (members // per_tile) + h][to, :] = joined[at : at + shells]
     left = jnp.concatenate([r[...].astype(BF16) for r in keep], axis=1)
     flat = shells * lats
+    copy.wait()
     for q in range(points // LANES):
         on = slice(q * LANES, (q + 1) * LANES)
         fc, fs = far_ref[0, :, q : q + 1], far_ref[1, :, q : q + 1]
@@ -378,10 +392,10 @@
     return pl.pallas_call(
         functools.partial(physical_body, orders),
         out_shape=jax.ShapeDtypeStruct(vorticity.shape, BF16),
-        in_specs=[vmem] * 4,
+        in_specs=[vmem, pl.BlockSpec(memory_space=pl.ANY), vmem, vmem],
         out_specs=vmem,
-        scratch_shapes=[pltpu.VMEM((3 * shells * lats, LANES), F32)]
-        * (2 * members * orders // LANES),
+        scratch_shapes=[pltpu.VMEM(vorticity.shape, BF16), pltpu.SemaphoreType.DMA((1,))]
+        + [pltpu.VMEM((3 * shells * lats, LANES), F32)] * (2 * members * orders // LANES),
         compiler_params=pltpu.CompilerParams(vmem_limit_bytes=40 * 2**20),
         name="physical",
     )(received, vorticity, near, far)
@@ -402,17 +416,12 @@
 
 
 def shards(groups, members, spectral, inverse, legendre, vorticity, degree_list, order_map):
-    width = spectral.shape[0]
     orders = spectral.shape[3]
     spec = jnp.transpose(spectral, (1, 2, 3, 4, 0))
     inv = jnp.transpose(inverse, (1, 2, 0))
     vort = jnp.transpose(vorticity, (0, 2, 1, 3))
-    degrees = lax.dynamic_slice_in_dim(degree_list, lax.axis_index("grp") * width, width)
-    orders_here = lax.dynamic_slice_in_dim(order_map, lax.axis_index("mem") * orders, orders)
     near, far = trig_tables(order_map, vorticity.shape[3])
-    partial = synthesize(
-        spec, inv, legendre, degrees.reshape(1, width), orders_here, groups, members
-    )
+    partial = synthesize(spec, inv, legendre, degree_list, order_map, groups, members)
     received = exchange(partial)
     out = physical(received, vort, near, far, orders)
     return jnp.transpose(out, (0, 2, 1, 3))
@@ -432,6 +441,8 @@
             and LANES < radii
             and 2 * radii == 3 * LANES
             and LANES % orders == 0
+            and orders % 2 == 0
+            and shells % 2 == 0
             and (shells // groups * 2) % 8 == 0
             and members % (LANES // orders) == 0
             and (lats // members) % (LANES // orders) == 0

time: 53.8 us -> 43.5 us (0.81)
  Pallas kernels: 49.2 us -> 40.8 us
  local copies, waits for them, and re-layouts: 3.12 us -> 1.27 us
    pallas_call x1, Pallas kernels: 27.8 us -> 19.1 us  [synthesize(): pl.pallas_call(functools.partial(synth_body, groups, members), out_shape=...]
    dynamic_slice x1 -> x0, local copies, waits for them, and re-layouts: 1.27 us -> none  [shards(): lax.dynamic_slice_in_dim(order_map, lax.axis_index('mem') * orders, orders)]
    reshape x1 -> x0, local copies, waits for them, and re-layouts: 0.58 us -> none  [shards(): degrees.reshape(1, width)]
    unnamed x8 -> x6, local copies, waits for them, and re-layouts: 1.28 us -> 1.27 us
where the time goes in v3:
time: 43.5 us; the launch traced here: 43.4 us
  Pallas kernels  40.8 us (94%)
  local copies, waits for them, and re-layouts  1.27 us (3%)
  other arithmetic  1.18 us (3%)
    pallas_call x1, Pallas kernels, synthesize(): pl.pallas_call(functools.partial(synth_body, groups, members), out_shape=...  19.1 us
    pallas_call x1, Pallas kernels, exchange(): pl.pallas_call(exchange_body, out_shape=jax.ShapeDtypeStruct((members, bl...  18.9 us
    pallas_call x1, Pallas kernels, physical(): pl.pallas_call(functools.partial(physical_body, orders), out_shape=jax.Sh...  2.87 us
    unnamed x6, local copies, waits for them, and re-layouts  1.27 us
    cos x1, other arithmetic, trig_tables(): jnp.cos(far)  1.14 us

profile of v3, /device:TPU:0, one launch (start us, length us, event | category | flops | bytes accessed | tf_op | source)
XLA Modules:
  0.0 43.4 jit_solution(8224617423038588077)
XLA Ops:
  0.0 0.0 copy-start.2
  0.0 19.1 %partial_sums.1.send_ref = bf16[8,2,2,144,128]{4,3,2,1,0:T(8,128)(2,1)} custom-call(bf16[3,2,32,192,128]{4,3,2,1,0:T(8,128)(2,1)} %bitcast.5, bf16[48,192,128]{2,1,0:T(8,128)(2,1)} %bitcast.6, bf16[32,64,128]{2,1,0:T(8,128)(2,1)} %leg_ref.1, s32[512]{0:T(512)} %deg_ref.1, s32[256]{0:T(256)} %ord_ref.1), custom_call_target="tpu_custom_call" | custom-call | tf_op jit(solution)/shard_map/partial_sums/pallas_call | solution.py:207
  19.1 0.0 copy-start
  19.1 1.3 %copy-done = bf16[8,2,2,144,128]{4,3,2,1,0:T(8,128)(2,1)S(1)} copy-done((bf16[8,2,2,144,128]{4,3,2,1,0:T(8,128)(2,1)S(1)}, bf16[8,2,2,144,128]{4,3,2,1,0:T(8,128)(2,1)}, u32[]{:S(2)}) %copy-start) | copy-done | bytes 1179672
  20.4 0.0 copy-start.1
  20.4 18.9 %exchange.1.recv_ref = bf16[8,144,128]{2,1,0:T(8,128)(2,1)S(1)} custom-call(bf16[8,2,2,144,128]{4,3,2,1,0:T(8,128)(2,1)S(1)} %copy-done), custom_call_target="tpu_custom_call" | custom-call | tf_op jit(solution)/shard_map/exchange/pallas_call | solution.py:330
  39.3 0.0 copy-done.2
  39.3 1.1 %fusion.7 = (f32[1,256,128]{2,1,0:T(8,128)S(1)}, f32[1,256,128]{2,1,0:T(8,128)S(1)}, f32[1,256,128]{2,1,0:T(8,128)S(1)}, f32[1,256,128]{2,1,0:T(8,128)S(1)}) fusion(s32[128]{0:T(128)S(1)} %iota_multiply_fusion, s32[256]{0:T(256)S(1)} %copy-done.2, f32[256]{0:T(256)S(1)} %compare_select_fusion), kind=kLoop, calls=%fused_computation.12 | loop fusion | flops 655360 | bytes 526848 | tf_op jit(solution)/shard_map/cos | solution.py:414
  40.5 0.0 copy-done.1
  40.5 2.9 %physical.1 = bf16[3,12,8,1536]{3,2,1,0:T(8,128)(2,1)} custom-call(bf16[8,144,128]{2,1,0:T(8,128)(2,1)S(1)} %exchange.1.recv_ref, bf16[3,12,8,1536]{3,2,1,0:T(8,128)(2,1)S(1)} %bitcast.4, f32[2,256,128]{2,1,0:T(8,128)S(1)} %get-tuple-element.11.near_ref, f32[2,256,128]{2,1,0:T(8,128)S(1)} %get-tuple-element.12.far_ref), custom_call_target="tpu_custom_call" | custom-call | tf_op jit(solution)/shard_map/physical/pallas_call | solution.py:392
  (3 shorter events, 0.0 us)
Async XLA Ops:
  0.0 39.3 %copy-start.2 = (s32[256]{0:T(256)S(1)}, s32[256]{0:T(256)}, u32[]{:S(2)}) copy-start(s32[256]{0:T(256)} %ord_ref.1) | copy-start | bytes 3076
  19.1 1.3 %copy-start = (bf16[8,2,2,144,128]{4,3,2,1,0:T(8,128)(2,1)S(1)}, bf16[8,2,2,144,128]{4,3,2,1,0:T(8,128)(2,1)}, u32[]{:S(2)}) copy-start(bf16[8,2,2,144,128]{4,3,2,1,0:T(8,128)(2,1)} %partial_sums.1.send_ref) | copy-start | bytes 3538948
  20.4 20.1 %copy-start.1 = (bf16[3,8,12,1536]{3,1,2,0:T(8,128)(2,1)S(1)}, bf16[3,8,12,1536]{3,1,2,0:T(8,128)(2,1)}, u32[]{:S(2)}) copy-start(bf16[3,8,12,1536]{3,1,2,0:T(8,128)(2,1)} %param.9) | copy-start | bytes 2654212

commit v4 on v1

v4 whole, which is shorter than its diff:
```python
import functools
import math

import jax
import jax.numpy as jnp
from jax import lax
from jax.experimental import pallas as pl
from jax.experimental.pallas import tpu as pltpu
from jax.sharding import PartitionSpec as P

F32 = jnp.float32
BF16 = jnp.bfloat16
LANES = 128
NT = (((1,), (1,)), ((), ()))
NN = (((1,), (0,)), ((), ()))


def nt(a, b):
    return lax.dot_general(a, b, NT, preferred_element_type=F32)


def nn(a, b):
    return lax.dot_general(a, b, NN, preferred_element_type=F32)


def cross_product(flow_velocity, vorticity):
    other = vorticity.astype(jnp.float32)
    first = flow_velocity[:, :, 1] * other[2] - flow_velocity[:, :, 2] * other[1]
    second = flow_velocity[:, :, 2] * other[0] - flow_velocity[:, :, 0] * other[2]
    third = flow_velocity[:, :, 0] * other[1] - flow_velocity[:, :, 1] * other[0]
    return jnp.stack([first, second, third]).astype(jnp.bfloat16)


def fourier_table(order_map, count):
    longitude = jnp.arange(count, dtype=jnp.int32)
    phase = order_map[:, None] * longitude[None, :] % count
    angle = phase.astype(jnp.float32) * (2.0 * math.pi / count)
    weight = jnp.where(order_map == 0, 1.0, 2.0).astype(jnp.float32)[:, None]
    return jnp.stack([weight * jnp.cos(angle), -weight * jnp.sin(angle)], axis=1).astype(
        jnp.bfloat16
    )


def plain_shards(spectral, inverse, legendre, vorticity, degree_list, order_map):
    orders = spectral.shape[3]
    shells = vorticity.shape[2]
    local_order_list = lax.dynamic_slice_in_dim(
        order_map, lax.axis_index("mem") * orders, orders
    )
    width = spectral.shape[0]
    flat = spectral.reshape(width, 6 * orders, spectral.shape[4])
    solved = lax.dot_general(
        inverse, flat, (((2,), (2,)), ((0,), (0,))), preferred_element_type=F32
    ).astype(BF16)
    moved = lax.all_to_all(solved, "grp", split_axis=1, concat_axis=0, tiled=True)
    by_order = jnp.transpose(
        moved.reshape(moved.shape[0], moved.shape[1] * 6, orders), (2, 0, 1)
    )
    segment = lax.all_gather(legendre, "grp", axis=2, tiled=True)
    allowed = local_order_list[:, None] <= degree_list[None, :]
    table = jnp.where(allowed[:, None, :], segment, jnp.zeros_like(segment))
    latitudinal = lax.dot_general(
        table, by_order, (((2,), (1,)), ((0,), (0,))), preferred_element_type=F32
    ).astype(BF16)
    gathered = lax.all_to_all(latitudinal, "mem", split_axis=1, concat_axis=0, tiled=True)
    arranged = gathered.reshape(gathered.shape[0], gathered.shape[1], shells, 3, 2)
    trig = fourier_table(order_map, vorticity.shape[3])
    velocity = jnp.einsum("mtsck,mkp->tscp", arranged, trig, preferred_element_type=F32)
    return cross_product(velocity, vorticity)


MESH = pl.DeviceIdType.MESH
CHUNKS = ((0, 1), (2,))
SLOTS = 6


def transfers(bufs, sems, send_ref, place):
    from_sib, to_far, from_far, to_mem, recv = bufs
    grp, me, core, sibling, across = place
    sib_s, sib_r, far_s, far_r, mem_s, mem_r = sems

    def to_sibling(j):
        return pltpu.make_async_remote_copy(
            src_ref=send_ref.at[j, 1 - core], dst_ref=from_sib.at[j],
            send_sem=sib_s.at[j], recv_sem=sib_r.at[j],
            device_id=(sibling, me), device_id_type=MESH,
        )

    def to_across(j):
        return pltpu.make_async_remote_copy(
            src_ref=to_far.at[j], dst_ref=from_far.at[j],
            send_sem=far_s.at[j], recv_sem=far_r.at[j],
            device_id=(across, me), device_id_type=MESH,
        )

    def to_member(j, slot):
        return pltpu.make_async_remote_copy(
            src_ref=to_mem.at[j], dst_ref=recv.at[slot],
            send_sem=mem_s.at[j], recv_sem=mem_r.at[slot],
            device_id=(grp, j), device_id_type=MESH,
        )

    return to_sibling, to_across, to_member


def synth_body(
    groups, members, spec_hbm, inv_hbm, leg_ref, deg_ref, ord_ref, *refs
):
    outs, refs = refs[: len(CHUNKS)], refs[len(CHUNKS) :]
    spec, inv, t0, t1, t2, main, rest, solved, f0, f1, f2, sems = refs[:12]
    refs = refs[12:]
    buffers = [refs[i * SLOTS : (i + 1) * SLOTS] for i in range(len(CHUNKS))]
    refs = refs[SLOTS * len(CHUNKS) :]
    sem_sets = [refs[i * 6 : (i + 1) * 6] for i in range(len(CHUNKS))]

    orders, radii, width = spec.shape[2:]
    shells = inv.shape[0]
    lats = leg_ref.shape[1]
    half = LANES // 2
    mine = shells // groups
    per_tile = LANES // orders
    pitch, lat_pitch = width + 1, orders + 1

    grp, me = lax.axis_index("grp"), lax.axis_index("mem")
    y, core = grp // 2, grp % 2
    sibling = y * 2 + (1 - core)
    across = (1 - y) * 2 + core
    place = (grp, me, core, sibling, across)

    barrier = pltpu.get_barrier_semaphore()
    for g in (sibling, across):
        pl.semaphore_signal(barrier, inc=1, device_id=(g, me), device_id_type=MESH)
    for i in range(1, members):
        pl.semaphore_signal(
            barrier, inc=1, device_id=(grp, (me + i) % members), device_id_type=MESH
        )

    inv_copy = pltpu.make_async_copy(inv_hbm, inv, sems.at[3])
    inv_copy.start()
    copies = [pltpu.make_async_copy(spec_hbm.at[c], spec.at[c], sems.at[c]) for c in range(3)]
    for copy in copies:
        copy.start()

    eye = (
        lax.broadcasted_iota(jnp.int32, (2 * width, 2 * width), 0)
        == lax.broadcasted_iota(jnp.int32, (2 * width, 2 * width), 1)
    ).astype(BF16)

    inv_copy.wait()

    def turn_inverse(i, carry):
        both = jnp.concatenate([inv[2 * i], inv[2 * i + 1]], axis=1)
        out = nt(eye, jnp.concatenate([both, both[LANES:]], axis=0))
        for h in range(2):
            at = pl.ds((2 * i + h) * pitch, width)
            part = out[h * width : (h + 1) * width]
            main[at, :] = part[:, 0:LANES]
            rest[at, :] = part[:, LANES : 2 * LANES]
        return carry

    lax.fori_loop(0, shells // 2, turn_inverse, 0, unroll=4)

    def turn(c):
        copies[c].wait()

        def turn_profiles(i, carry):
            a, b = [
                jnp.concatenate([spec[c, k, 2 * i], spec[c, k, 2 * i + 1]], axis=1)
                for k in range(2)
            ]
            out = nt(eye, jnp.concatenate([a, b[LANES:], b[:LANES]], axis=0))
            for h in range(2):
                at = pl.ds((c * orders + 2 * i + h) * pitch, width)
                part = out[h * width : (h + 1) * width]
                t0[at, :] = part[:, 0:LANES]
                t1[at, :] = part[:, LANES : 2 * LANES]
                t2[at, :] = part[:, 2 * LANES : 3 * LANES]
            return carry

        lax.fori_loop(0, orders // 2, turn_profiles, 0, unroll=4)

    nothing = jnp.zeros((shells, LANES), BF16)
    pad = jnp.zeros((half - shells, 3 * LANES), BF16)
    low = lax.broadcasted_iota(jnp.int32, (shells, LANES), 1) < half

    def solve_chunk(comps):
        def solve(l, carry):
            at = pl.ds(comps[0] * orders * pitch + l, len(comps) * orders, stride=pitch)
            profiles = jnp.concatenate([r[at, :].astype(BF16) for r in (t0, t1, t2)], axis=1)
            on = pl.ds(l, shells, stride=pitch)
            first, last = main[on, :].astype(BF16), rest[on, :]
            lower = jnp.where(low, last, 0.0).astype(BF16)
            upper = jnp.where(low, 0.0, last).astype(BF16)
            real = jnp.concatenate([first, lower, nothing], axis=1)
            imag = jnp.concatenate([nothing, upper, first], axis=1)
            solved[at, :] = nt(profiles, jnp.concatenate([real, pad, imag, pad], axis=0))
            return carry

        lax.fori_loop(0, width, solve, 0, unroll=16)

    degrees = deg_ref[pl.ds(pl.multiple_of(grp * width, width), width)].reshape(1, width)
    sums = (f0, f1, f2)

    def sum_chunk(comps):
        def sum_degrees(m, carry):
            valid = degrees >= ord_ref[me * orders + m]
            table = jnp.where(valid, leg_ref[m].astype(F32), 0.0).astype(BF16)
            block = jnp.concatenate(
                [
                    solved[pl.ds((c * orders + m) * pitch, width), :].astype(BF16)
                    for c in comps
                ],
                axis=1,
            )
            out = nn(table, block)
            at = pl.ds(m, lats, stride=lat_pitch)
            for i, c in enumerate(comps):
                sums[c][at, :] = out[:, i * LANES : (i + 1) * LANES]
            return carry

        lax.fori_loop(0, orders, sum_degrees, 0, unroll=8)

    row = lax.broadcasted_iota(jnp.int32, (2 * shells, LANES), 0)
    lane = lax.broadcasted_iota(jnp.int32, (2 * shells, LANES), 1)
    want = row
    for i in range(1, 2 * groups):
        g, k = i // 2, i % 2
        step = (half + g * mine - i * mine) if k else (g * mine - i * mine)
        want = jnp.where(row >= i * mine, row + step, want)
    pick = (want == lane).astype(BF16)
    tiles = lats // members // per_tile

    def target(i):
        return (me + 1 + i) % members

    def send_chunk(n):
        send_ref = buffers[n][0]
        to_sibling, _, _ = transfers(buffers[n][1:], sem_sets[n], send_ref, place)

        def turn_sums(i, carry):
            j = target(i)
            parts = []
            for b in range(tiles):
                at = [
                    pl.ds(((j * tiles + b) * per_tile + i) * lat_pitch, orders)
                    for i in range(per_tile)
                ]
                for c in CHUNKS[n]:
                    both = jnp.concatenate([sums[c][a, :].astype(BF16) for a in at], axis=0)
                    parts.append(nt(pick, both))
            for g in range(groups):
                block = [p[g * 2 * mine : (g + 1) * 2 * mine] for p in parts]
                send_ref[j, g % 2, g // 2] = jnp.concatenate(block, axis=0).astype(BF16)
            to_sibling(j).start()
            return carry

        lax.fori_loop(0, members, turn_sums, 0)

    def pair_sum(n, j, which):
        send_ref, from_sib = buffers[n][:2]
        return send_ref[j, core, which].astype(F32) + from_sib[j, which].astype(F32)

    def second(n):
        to_sibling, to_across, _ = transfers(buffers[n][1:], sem_sets[n], buffers[n][0], place)
        to_far = buffers[n][2]

        def step(i, carry):
            j = target(i)
            to_sibling(j).wait_recv()
            to_far[j] = pair_sum(n, j, 1 - y).astype(BF16)
            to_across(j).start()
            return carry

        lax.fori_loop(0, members, step, 0)

    def third(n):
        _, to_across, to_member = transfers(buffers[n][1:], sem_sets[n], buffers[n][0], place)
        _, _, _, from_far, to_mem, _ = buffers[n]

        def total(j):
            to_across(j).wait_recv()
            return (pair_sum(n, j, y) + from_far[j].astype(F32)).astype(BF16)

        def step(i, carry):
            j = target(i)
            to_mem[j] = total(j)
            to_member(j, me).start()
            return carry

        lax.fori_loop(0, members - 1, step, 0)
        outs[n][me] = total(me)

    def finish(n):
        moves = transfers(buffers[n][1:], sem_sets[n], buffers[n][0], place)
        to_sibling, to_across, to_member = moves
        recv = buffers[n][5]

        def step(i, carry):
            j = target(i)
            to_member(j, j).wait_recv()
            outs[n][j] = recv[j]
            to_member(j, me).wait_send()
            return carry

        lax.fori_loop(0, members - 1, step, 0)

        def drain(i, carry):
            to_sibling(i).wait_send()
            to_across(i).wait_send()
            return carry

        lax.fori_loop(0, members, drain, 0)

    last = len(CHUNKS) - 1
    for n, comps in enumerate(CHUNKS):
        for c in comps:
            turn(c)
        if n:
            second(n - 1)
        solve_chunk(comps)
        if n:
            third(n - 1)
        sum_chunk(comps)
        if n == 0:
            pl.semaphore_wait(barrier, members + 1)
        send_chunk(n)
    second(last)
    third(last)
    for n in range(len(CHUNKS)):
        finish(n)


def synthesize(spec, inv, legendre, degree_list, order_map, groups, members):
    _, _, orders, radii, width = spec.shape
    shells = inv.shape[0]
    lats = legendre.shape[1]
    mine = shells // groups
    pitch = width + 1
    any_space = pl.BlockSpec(memory_space=pl.ANY)
    vmem = pl.BlockSpec(memory_space=pltpu.VMEM)
    buffers, shapes = [], []
    for comps in CHUNKS:
        block = lats // members * orders * mine * 2 * len(comps) // LANES
        slots = pltpu.VMEM((members, block, LANES), BF16)
        buffers += [
            pltpu.VMEM((members, 2, groups // 2, block, LANES), BF16),
            pltpu.VMEM((members, groups // 2, block, LANES), BF16),
            slots, slots, slots, slots,
        ]
        shapes.append(jax.ShapeDtypeStruct((members, block, LANES), BF16))
    return pl.pallas_call(
        functools.partial(synth_body, groups, members),
        out_shape=shapes,
        in_specs=[any_space, any_space, vmem, vmem, pl.BlockSpec(memory_space=pltpu.SMEM)],
        out_specs=[vmem] * len(CHUNKS),
        scratch_shapes=[
            pltpu.VMEM(spec.shape, BF16),
            pltpu.VMEM(inv.shape, BF16),
            *[pltpu.VMEM((3 * orders * pitch, LANES), F32)] * 3,
            *[pltpu.VMEM((shells * pitch, LANES), F32)] * 2,
            pltpu.VMEM((3 * orders * pitch, LANES), F32),
            *[pltpu.VMEM((lats * (orders + 1), LANES), F32)] * 3,
            pltpu.SemaphoreType.DMA((4,)),
            *buffers,
            *[pltpu.SemaphoreType.DMA((members,))] * (6 * len(CHUNKS)),
        ],
        compiler_params=pltpu.CompilerParams(
            collective_id=0, has_side_effects=True, vmem_limit_bytes=60 * 2**20
        ),
        name="synthesize",
    )(spec, inv, legendre, degree_list, order_map)


def cos_sin(phase, count):
    phase = phase - count * jnp.floor((phase + 0.5) * (1.0 / count))
    turns = jnp.floor((phase + count / 8) * (4.0 / count))
    t = (phase - turns * (count / 4)) * (2.0 * math.pi / count)
    x = t * t
    s = t * (1 + x * (-1 / 6 + x * (1 / 120 + x * (-1 / 5040 + x * (1 / 362880)))))
    c = 1 + x * (
        -1 / 2 + x * (1 / 24 + x * (-1 / 720 + x * (1 / 40320 + x * (-1 / 3628800))))
    )
    odd = (turns == 1) | (turns == 3)
    cos, sin = jnp.where(odd, s, c), jnp.where(odd, c, s)
    cos = jnp.where((turns == 1) | (turns == 2), -cos, cos)
    sin = jnp.where((turns == 2) | (turns == 3), -sin, sin)
    return cos, sin


def physical_body(orders, *refs):
    recvs, refs = refs[: len(CHUNKS)], refs[len(CHUNKS) :]
    vort_hbm, ord_ref, out_ref, vort_ref, sem, *keep = refs
    copy = pltpu.make_async_copy(vort_hbm, vort_ref, sem.at[0])
    copy.start()
    members = recvs[0].shape[0]
    shells = vort_ref.shape[1]
    lats = vort_ref.shape[2]
    points = vort_ref.shape[3]
    every = members * orders
    per_tile = LANES // orders
    tiles = lats // per_tile
    for comps, recv_ref in zip(CHUNKS, recvs):
        for i in range(per_tile):
            for h in range(members // per_tile):
                parts = [
                    recv_ref[h * per_tile + j].astype(F32)[:, i * orders : (i + 1) * orders]
                    for j in range(per_tile)
                ]
                joined = jnp.concatenate(parts, axis=1)
                for b in range(tiles):
                    for n, c in enumerate(comps):
                        for k in range(2):
                            at = ((b * len(comps) + n) * 2 + k) * shells
                            to = pl.ds(
                                c * shells * lats + b * per_tile + i, shells, stride=lats
                            )
                            keep[k * (members // per_tile) + h][to, :] = joined[at : at + shells]
    left = jnp.concatenate([r[...].astype(BF16) for r in keep], axis=1)

    line = ord_ref[...].reshape(1, every).astype(F32)
    same = lax.broadcasted_iota(jnp.int32, (every, every), 0) == lax.broadcasted_iota(
        jnp.int32, (every, every), 1
    )
    column = jnp.sum(jnp.where(same, line, 0.0), axis=1, keepdims=True)
    lane = lax.broadcasted_iota(jnp.int32, (every, LANES), 1).astype(F32)
    nc, ns = cos_sin(column * lane, points)
    weight = jnp.where(column == 0.0, 1.0, 2.0)
    nc, ns = weight * nc, weight * ns
    far_c, far_s = cos_sin(column * (lane * LANES), points)

    flat = shells * lats
    copy.wait()
    for q in range(points // LANES):
        on = slice(q * LANES, (q + 1) * LANES)
        fc, fs = far_c[:, q : q + 1], far_s[:, q : q + 1]
        trig = jnp.concatenate([nc * fc - ns * fs, -(ns * fc + nc * fs)], axis=0).astype(BF16)
        v = nn(left, trig)
        v0, v1, v2 = v[:flat], v[flat : 2 * flat], v[2 * flat :]
        w0, w1, w2 = [vort_ref[c, :, :, on].reshape(flat, LANES).astype(F32) for c in range(3)]
        shape = (shells, lats, LANES)
        out_ref[0, :, :, on] = (v1 * w2 - v2 * w1).astype(BF16).reshape(shape)
        out_ref[1, :, :, on] = (v2 * w0 - v0 * w2).astype(BF16).reshape(shape)
        out_ref[2, :, :, on] = (v0 * w1 - v1 * w0).astype(BF16).reshape(shape)


def physical(received, vorticity, order_map, orders):
    members = received[0].shape[0]
    _, shells, lats, _ = vorticity.shape
    vmem = pl.BlockSpec(memory_space=pltpu.VMEM)
    return pl.pallas_call(
        functools.partial(physical_body, orders),
        out_shape=jax.ShapeDtypeStruct(vorticity.shape, BF16),
        in_specs=[vmem] * len(CHUNKS) + [pl.BlockSpec(memory_space=pl.ANY), vmem],
        out_specs=vmem,
        scratch_shapes=[pltpu.VMEM(vorticity.shape, BF16), pltpu.SemaphoreType.DMA((1,))]
        + [pltpu.VMEM((3 * shells * lats, LANES), F32)] * (2 * members * orders // LANES),
        compiler_params=pltpu.CompilerParams(vmem_limit_bytes=40 * 2**20),
        name="physical",
    )(*received, vorticity, order_map)


def shards(groups, members, spectral, inverse, legendre, vorticity, degree_list, order_map):
    orders = spectral.shape[3]
    spec = jnp.transpose(spectral, (1, 2, 3, 4, 0))
    inv = jnp.transpose(inverse, (1, 2, 0))
    vort = jnp.transpose(vorticity, (0, 2, 1, 3))
    received = synthesize(spec, inv, legendre, degree_list, order_map, groups, members)
    out = physical(received, vort, order_map, orders)
    return jnp.transpose(out, (0, 2, 1, 3))


def solution(mesh):
    groups, members = mesh.shape["grp"], mesh.shape["mem"]

    def local(spectral, inverse, legendre, vorticity, degree_list, order_map):
        args = (spectral, inverse, legendre, vorticity, degree_list, order_map)
        width, _, _, orders, radii = spectral.shape
        shells, lats = inverse.shape[1], legendre.shape[1]
        fits = (
            groups == 4
            and width == LANES
            and 2 * shells <= LANES
            and LANES < radii
            and 2 * radii == 3 * LANES
            and LANES % orders == 0
            and orders % 2 == 0
            and shells % 2 == 0
            and (shells // groups * 2) % 8 == 0
            and members % (LANES // orders) == 0
            and (lats // members) % (LANES // orders) == 0
            and vorticity.shape[3] % LANES == 0
            and vorticity.shape[3] // LANES <= LANES
            and members * orders * vorticity.shape[3] < 2**23
            and (lats // members) * orders * (shells // groups) * 2 % (16 * LANES) == 0
        )
        if fits:
            return shards(groups, members, *args)
        return plain_shards(*args)

    return jax.shard_map(
        local,
        mesh=mesh,
        in_specs=(
            P("grp", None, None, "mem", None),
            P("grp", None, None),
            P("mem", None, "grp"),
            P(None, "mem", "grp", None),
            P(),
            P(),
        ),
        out_specs=P(None, "mem", "grp", None),
        check_vma=False,
    )
```

time: 116 us -> 44.1 us (0.38)
  waiting for transfers between devices: 37 us -> 0 us
  between operations: 13.5 us -> 0.04 us
  Pallas kernels: 54.4 us -> 42.1 us
  starting transfers between devices: 5.49 us -> 0 us
  local copies, waits for them, and re-layouts: 4.36 us -> 1.82 us
  other arithmetic: 1.18 us -> 0 us
    reduce_scatter x1 -> x0, waiting for transfers between devices: 28.6 us -> none  [shards(): summed = lax.psum_scatter(partial, 'grp', scatter_dimension=1, tiled=False)]
    pallas_call x1, Pallas kernels: 51.6 us -> 38.8 us  [synthesize(): pl.pallas_call(functools.partial(synth_body, groups, members), out_shape=...]
    all_to_all x1 -> x0, waiting for transfers between devices: 8.42 us -> none  [shards(): lax.all_to_all(summed, 'mem', split_axis=0, concat_axis=0, tiled=True)]
    all_to_all x1 -> x0, starting transfers between devices: 5.49 us -> none  [shards(): lax.all_to_all(summed, 'mem', split_axis=0, concat_axis=0, tiled=True)]
    pallas_call x1 -> x0, local copies, waits for them, and re-layouts: 2.45 us -> none  [synthesize(): pl.pallas_call(functools.partial(synth_body, groups, members), out_shape=...]
    unnamed x6 -> x8, local copies, waits for them, and re-layouts: 0.02 us -> 1.82 us
    dynamic_slice x1 -> x0, local copies, waits for them, and re-layouts: 1.3 us -> none  [shards(): lax.dynamic_slice_in_dim(order_map, lax.axis_index('mem') * orders, orders)]
  transfers between devices with their start and end apart: 2 -> 0, of which waited for: 2 -> 0; matrix products, arithmetic and copies ran while one was open for 1% -> 0% of each run, Pallas kernels for 0% -> 0%
where the time goes in v4:
time: 44.1 us; the launch traced here: 43.9 us
  Pallas kernels  42.1 us (95%)
  local copies, waits for them, and re-layouts  1.82 us (4%)
    pallas_call x1, Pallas kernels, synthesize(): pl.pallas_call(functools.partial(synth_body, groups, members), out_shape=...  38.8 us
    pallas_call x1, Pallas kernels, physical(): pl.pallas_call(functools.partial(physical_body, orders), out_shape=jax.Sh...  3.26 us
    unnamed x8, local copies, waits for them, and re-layouts  1.82 us

profile of v4, /device:TPU:0, one launch (start us, length us, event | category | flops | bytes accessed | tf_op | source)
XLA Modules:
  0.0 43.9 jit_solution(4782727819413193557)
XLA Ops:
  0.0 0.0 copy-start.3
  0.0 0.0 copy-start
  0.0 38.8 %synthesize.1 = (bf16[8,96,128]{2,1,0:T(8,128)(2,1)}, bf16[8,48,128]{2,1,0:T(8,128)(2,1)}) custom-call(bf16[3,2,32,192,128]{4,3,2,1,0:T(8,128)(2,1)} %bitcast.5, bf16[48,192,128]{2,1,0:T(8,128)(2,1)} %bitcast.6, bf16[32,64,128]{2,1,0:T(8,128)(2,1)} %leg_ref.1, s32[512]{0:T(512)} %deg_ref.1, s32[256]{0:T(256)} %refs_3_.1), custom_call_target="tpu_custom_call" | custom-call | tf_op jit(solution)/shard_map/synthesize/pallas_call | solution.py:351
  38.8 0.0 copy-done.3
  38.8 0.0 copy-done
  38.9 0.0 copy-start.1
  38.9 0.9 %copy-done.1 = bf16[8,96,128]{2,1,0:T(8,128)(2,1)S(1)} copy-done((bf16[8,96,128]{2,1,0:T(8,128)(2,1)S(1)}, bf16[8,96,128]{2,1,0:T(8,128)(2,1)}, u32[]{:S(2)}) %copy-start.1) | copy-done | bytes 196632
  39.8 0.0 copy-start.2
  39.8 0.9 %copy-done.2 = bf16[8,48,128]{2,1,0:T(8,128)(2,1)S(1)} copy-done((bf16[8,48,128]{2,1,0:T(8,128)(2,1)S(1)}, bf16[8,48,128]{2,1,0:T(8,128)(2,1)}, u32[]{:S(2)}) %copy-start.2) | copy-done | bytes 98328
  40.7 3.3 %physical.1 = bf16[3,12,8,1536]{3,2,1,0:T(8,128)(2,1)} custom-call(bf16[8,96,128]{2,1,0:T(8,128)(2,1)S(1)} %copy-done.1, bf16[8,48,128]{2,1,0:T(8,128)(2,1)S(1)} %copy-done.2, bf16[3,12,8,1536]{3,2,1,0:T(8,128)(2,1)S(1)} %bitcast.4, s32[256]{0:T(256)S(1)} %copy-done.3), custom_call_target="tpu_custom_call" | custom-call | tf_op jit(solution)/shard_map/physical/pallas_call | solution.py:450
Async XLA Ops:
  0.0 38.8 %copy-start.3 = (s32[256]{0:T(256)S(1)}, s32[256]{0:T(256)}, u32[]{:S(2)}) copy-start(s32[256]{0:T(256)} %refs_3_.1) | copy-start | bytes 3076
  0.0 38.8 %copy-start = (bf16[3,8,12,1536]{3,1,2,0:T(8,128)(2,1)S(1)}, bf16[3,8,12,1536]{3,1,2,0:T(8,128)(2,1)}, u32[]{:S(2)}) copy-start(bf16[3,8,12,1536]{3,1,2,0:T(8,128)(2,1)} %param.9) | copy-start | bytes 2654212
  38.9 0.9 %copy-start.1 = (bf16[8,96,128]{2,1,0:T(8,128)(2,1)S(1)}, bf16[8,96,128]{2,1,0:T(8,128)(2,1)}, u32[]{:S(2)}) copy-start(bf16[8,96,128]{2,1,0:T(8,128)(2,1)} %get-tuple-element.7.refs_0_) | copy-start | bytes 589828
  39.8 0.9 %copy-start.2 = (bf16[8,48,128]{2,1,0:T(8,128)(2,1)S(1)}, bf16[8,48,128]{2,1,0:T(8,128)(2,1)}, u32[]{:S(2)}) copy-start(bf16[8,48,128]{2,1,0:T(8,128)(2,1)} %get-tuple-element.8.refs_1_) | copy-start | bytes 294916

commit v5 on v4

--- a/solution.py
+++ b/solution.py
@@ -104,11 +104,11 @@
 
 
 def synth_body(
-    groups, members, spec_hbm, inv_hbm, leg_ref, deg_ref, ord_ref, *refs
+    groups, members, spec_hbm, inv_hbm, leg_hbm, deg_ref, ord_ref, *refs
 ):
     outs, refs = refs[: len(CHUNKS)], refs[len(CHUNKS) :]
-    spec, inv, t0, t1, t2, main, rest, solved, f0, f1, f2, sems = refs[:12]
-    refs = refs[12:]
+    spec, inv, leg_ref, t0, t1, t2, main, rest, solved, f0, f1, f2, sems = refs[:13]
+    refs = refs[13:]
     buffers = [refs[i * SLOTS : (i + 1) * SLOTS] for i in range(len(CHUNKS))]
     refs = refs[SLOTS * len(CHUNKS) :]
     sem_sets = [refs[i * 6 : (i + 1) * 6] for i in range(len(CHUNKS))]
@@ -138,7 +138,8 @@
     inv_copy = pltpu.make_async_copy(inv_hbm, inv, sems.at[3])
     inv_copy.start()
     copies = [pltpu.make_async_copy(spec_hbm.at[c], spec.at[c], sems.at[c]) for c in range(3)]
-    for copy in copies:
+    leg_copy = pltpu.make_async_copy(leg_hbm, leg_ref, sems.at[4])
+    for copy in (*copies, leg_copy):
         copy.start()
 
     eye = (
@@ -179,21 +180,22 @@
 
         lax.fori_loop(0, orders // 2, turn_profiles, 0, unroll=4)
 
-    nothing = jnp.zeros((shells, LANES), BF16)
-    pad = jnp.zeros((half - shells, 3 * LANES), BF16)
-    low = lax.broadcasted_iota(jnp.int32, (shells, LANES), 1) < half
+    pad = jnp.zeros((half - shells, 2 * LANES), BF16)
 
     def solve_chunk(comps):
+        count = len(comps) * orders
+        low = lax.broadcasted_iota(jnp.int32, (count, LANES), 1) < half
+
         def solve(l, carry):
-            at = pl.ds(comps[0] * orders * pitch + l, len(comps) * orders, stride=pitch)
-            profiles = jnp.concatenate([r[at, :].astype(BF16) for r in (t0, t1, t2)], axis=1)
+            at = pl.ds(comps[0] * orders * pitch + l, count, stride=pitch)
+            shared = t1[at, :]
+            real = jnp.concatenate([t0[at, :], jnp.where(low, shared, 0.0)], axis=1)
+            imag = jnp.concatenate([t2[at, :], jnp.where(low, 0.0, shared)], axis=1)
+            profiles = jnp.concatenate([real, imag], axis=0).astype(BF16)
             on = pl.ds(l, shells, stride=pitch)
-            first, last = main[on, :].astype(BF16), rest[on, :]
-            lower = jnp.where(low, last, 0.0).astype(BF16)
-            upper = jnp.where(low, 0.0, last).astype(BF16)
-            real = jnp.concatenate([first, lower, nothing], axis=1)
-            imag = jnp.concatenate([nothing, upper, first], axis=1)
-            solved[at, :] = nt(profiles, jnp.concatenate([real, pad, imag, pad], axis=0))
+            weights = jnp.concatenate([main[on, :], rest[on, :]], axis=1).astype(BF16)
+            out = nt(profiles, jnp.concatenate([weights, pad], axis=0))
+            solved[at, :] = jnp.concatenate([out[:count], out[count:]], axis=1)
             return carry
 
         lax.fori_loop(0, width, solve, 0, unroll=16)
@@ -254,7 +256,7 @@
             to_sibling(j).start()
             return carry
 
-        lax.fori_loop(0, members, turn_sums, 0)
+        lax.fori_loop(0, members, turn_sums, 0, unroll=2)
 
     def pair_sum(n, j, which):
         send_ref, from_sib = buffers[n][:2]
@@ -320,6 +322,8 @@
         solve_chunk(comps)
         if n:
             third(n - 1)
+        if n == 0:
+            leg_copy.wait()
         sum_chunk(comps)
         if n == 0:
             pl.semaphore_wait(barrier, members + 1)
@@ -351,21 +355,22 @@
     return pl.pallas_call(
         functools.partial(synth_body, groups, members),
         out_shape=shapes,
-        in_specs=[any_space, any_space, vmem, vmem, pl.BlockSpec(memory_space=pltpu.SMEM)],
+        in_specs=[any_space] * 3 + [vmem, pl.BlockSpec(memory_space=pltpu.SMEM)],
         out_specs=[vmem] * len(CHUNKS),
         scratch_shapes=[
             pltpu.VMEM(spec.shape, BF16),
             pltpu.VMEM(inv.shape, BF16),
+            pltpu.VMEM(legendre.shape, BF16),
             *[pltpu.VMEM((3 * orders * pitch, LANES), F32)] * 3,
             *[pltpu.VMEM((shells * pitch, LANES), F32)] * 2,
             pltpu.VMEM((3 * orders * pitch, LANES), F32),
             *[pltpu.VMEM((lats * (orders + 1), LANES), F32)] * 3,
-            pltpu.SemaphoreType.DMA((4,)),
+            pltpu.SemaphoreType.DMA((5,)),
             *buffers,
             *[pltpu.SemaphoreType.DMA((members,))] * (6 * len(CHUNKS)),
         ],
         compiler_params=pltpu.CompilerParams(
-            collective_id=0, has_side_effects=True, vmem_limit_bytes=60 * 2**20
+            collective_id=0, has_side_effects=True, vmem_limit_bytes=52 * 2**20
         ),
         name="synthesize",
     )(spec, inv, legendre, degree_list, order_map)
@@ -390,7 +395,13 @@
 def physical_body(orders, *refs):
     recvs, refs = refs[: len(CHUNKS)], refs[len(CHUNKS) :]
     vort_hbm, ord_ref, out_ref, vort_ref, sem, *keep = refs
+    held, keep = keep[: len(CHUNKS)], keep[len(CHUNKS) :]
     copy = pltpu.make_async_copy(vort_hbm, vort_ref, sem.at[0])
+    arrivals = [
+        pltpu.make_async_copy(r, h, sem.at[1 + n]) for n, (r, h) in enumerate(zip(recvs, held))
+    ]
+    for arrival in arrivals:
+        arrival.start()
     copy.start()
     members = recvs[0].shape[0]
     shells = vort_ref.shape[1]
@@ -399,7 +410,20 @@
     every = members * orders
     per_tile = LANES // orders
     tiles = lats // per_tile
-    for comps, recv_ref in zip(CHUNKS, recvs):
+    line = ord_ref[...].reshape(1, every).astype(F32)
+    same = lax.broadcasted_iota(jnp.int32, (every, every), 0) == lax.broadcasted_iota(
+        jnp.int32, (every, every), 1
+    )
+    column = jnp.sum(jnp.where(same, line, 0.0), axis=1, keepdims=True)
+    lane = lax.broadcasted_iota(jnp.int32, (every, LANES), 1).astype(F32)
+    nc, ns = cos_sin(column * lane, points)
+    weight = jnp.where(column == 0.0, 1.0, 2.0)
+    nc, ns = weight * nc, weight * ns
+    far_c, far_s = cos_sin(column * (lane * LANES), points)
+
+    for arrival in arrivals:
+        arrival.wait()
+    for comps, recv_ref in zip(CHUNKS, held):
         for i in range(per_tile):
             for h in range(members // per_tile):
                 parts = [
@@ -417,17 +441,6 @@
                             keep[k * (members // per_tile) + h][to, :] = joined[at : at + shells]
     left = jnp.concatenate([r[...].astype(BF16) for r in keep], axis=1)
 
-    line = ord_ref[...].reshape(1, every).astype(F32)
-    same = lax.broadcasted_iota(jnp.int32, (every, every), 0) == lax.broadcasted_iota(
-        jnp.int32, (every, every), 1
-    )
-    column = jnp.sum(jnp.where(same, line, 0.0), axis=1, keepdims=True)
-    lane = lax.broadcasted_iota(jnp.int32, (every, LANES), 1).astype(F32)
-    nc, ns = cos_sin(column * lane, points)
-    weight = jnp.where(column == 0.0, 1.0, 2.0)
-    nc, ns = weight * nc, weight * ns
-    far_c, far_s = cos_sin(column * (lane * LANES), points)
-
     flat = shells * lats
     copy.wait()
     for q in range(points // LANES):
@@ -450,11 +463,15 @@
     return pl.pallas_call(
         functools.partial(physical_body, orders),
         out_shape=jax.ShapeDtypeStruct(vorticity.shape, BF16),
-        in_specs=[vmem] * len(CHUNKS) + [pl.BlockSpec(memory_space=pl.ANY), vmem],
+        in_specs=[pl.BlockSpec(memory_space=pl.ANY)] * (len(CHUNKS) + 1) + [vmem],
         out_specs=vmem,
-        scratch_shapes=[pltpu.VMEM(vorticity.shape, BF16), pltpu.SemaphoreType.DMA((1,))]
+        scratch_shapes=[
+            pltpu.VMEM(vorticity.shape, BF16),
+            pltpu.SemaphoreType.DMA((1 + len(CHUNKS),)),
+        ]
+        + [pltpu.VMEM(r.shape, BF16) for r in received]
         + [pltpu.VMEM((3 * shells * lats, LANES), F32)] * (2 * members * orders // LANES),
-        compiler_params=pltpu.CompilerParams(vmem_limit_bytes=40 * 2**20),
+        compiler_params=pltpu.CompilerParams(vmem_limit_bytes=24 * 2**20),
         name="physical",
     )(*received, vorticity, order_map)
 

time: 44.1 us -> 42.2 us (0.957)
  Pallas kernels: 42.1 us -> 39.5 us
  local copies, waits for them, and re-layouts: 1.82 us -> 2.48 us
    pallas_call x1, Pallas kernels: 38.8 us -> 35.8 us  [synthesize(): pl.pallas_call(functools.partial(synth_body, groups, members), out_shape=...]
    unnamed x8, local copies, waits for them, and re-layouts: 1.82 us -> 2.48 us
    pallas_call x1, Pallas kernels: 3.26 us -> 3.72 us  [physical(): pl.pallas_call(functools.partial(physical_body, orders), out_shape=jax.Sh...]
where the time goes in v5:
time: 42.2 us; the launch traced here: 42 us
  Pallas kernels  39.5 us (94%)
  local copies, waits for them, and re-layouts  2.48 us (6%)
    pallas_call x1, Pallas kernels, synthesize(): pl.pallas_call(functools.partial(synth_body, groups, members), out_shape=...  35.8 us
    pallas_call x1, Pallas kernels, physical(): pl.pallas_call(functools.partial(physical_body, orders), out_shape=jax.Sh...  3.72 us
    unnamed x8, local copies, waits for them, and re-layouts  2.48 us

profile of v5, /device:TPU:0, one launch (start us, length us, event | category | flops | bytes accessed | tf_op | source)
XLA Modules:
  0.0 42.0 jit_solution(8099898979214896969)
XLA Ops:
  0.0 0.0 copy-start
  0.0 0.0 copy-start.1
  0.0 1.1 %copy-done.1 = bf16[32,64,128]{2,1,0:T(8,128)(2,1)S(1)} copy-done((bf16[32,64,128]{2,1,0:T(8,128)(2,1)S(1)}, bf16[32,64,128]{2,1,0:T(8,128)(2,1)}, u32[]{:S(2)}) %copy-start.1) | copy-done | bytes 524312
  1.1 0.0 copy-start.2
  1.1 0.7 %copy-done.2 = s32[256]{0:T(256)S(1)} copy-done((s32[256]{0:T(256)S(1)}, s32[256]{0:T(256)}, u32[]{:S(2)}) %copy-start.2) | copy-done | bytes 1048
  1.8 0.0 copy-start.3
  1.8 0.7 %copy-done.3 = s32[512]{0:T(512)S(1)} copy-done((s32[512]{0:T(512)S(1)}, s32[512]{0:T(512)}, u32[]{:S(2)}) %copy-start.3) | copy-done | bytes 2072
  2.5 35.8 %synthesize.1 = (bf16[8,96,128]{2,1,0:T(8,128)(2,1)S(1)}, bf16[8,48,128]{2,1,0:T(8,128)(2,1)S(1)}) custom-call(bf16[3,2,32,192,128]{4,3,2,1,0:T(8,128)(2,1)} %bitcast.5, bf16[48,192,128]{2,1,0:T(8,128)(2,1)} %bitcast.6, bf16[32,64,128]{2,1,0:T(8,128)(2,1)S(1)} %copy-done.1, s32[512]{0:T(512)S(1)} %copy-done.3, s32[256]{0:T(256)S(1)} %copy-done.2), custom_call_target="tpu_custom_call" | custom-call | tf_op jit(solution)/shard_map/synthesize/pallas_call | solution.py:355
  38.3 0.0 copy-done
  38.3 3.7 %physical.1 = bf16[3,12,8,1536]{3,2,1,0:T(8,128)(2,1)} custom-call(bf16[8,96,128]{2,1,0:T(8,128)(2,1)S(1)} %get-tuple-element.7.refs_0_, bf16[8,48,128]{2,1,0:T(8,128)(2,1)S(1)} %get-tuple-element.8.refs_1_, bf16[3,12,8,1536]{3,2,1,0:T(8,128)(2,1)S(1)} %bitcast.4, s32[256]{0:T(256)S(1)} %copy-done.2), custom_call_target="tpu_custom_call" | custom-call | tf_op jit(solution)/shard_map/physical/pallas_call | solution.py:463
Async XLA Ops:
  0.0 38.3 %copy-start = (bf16[3,8,12,1536]{3,1,2,0:T(8,128)(2,1)S(1)}, bf16[3,8,12,1536]{3,1,2,0:T(8,128)(2,1)}, u32[]{:S(2)}) copy-start(bf16[3,8,12,1536]{3,1,2,0:T(8,128)(2,1)} %param.9) | copy-start | bytes 2654212
  0.0 1.1 %copy-start.1 = (bf16[32,64,128]{2,1,0:T(8,128)(2,1)S(1)}, bf16[32,64,128]{2,1,0:T(8,128)(2,1)}, u32[]{:S(2)}) copy-start(bf16[32,64,128]{2,1,0:T(8,128)(2,1)} %leg_hbm.1) | copy-start | bytes 1572868
  1.1 0.7 %copy-start.2 = (s32[256]{0:T(256)S(1)}, s32[256]{0:T(256)}, u32[]{:S(2)}) copy-start(s32[256]{0:T(256)} %refs_3_.1) | copy-start | bytes 3076
  1.8 0.7 %copy-start.3 = (s32[512]{0:T(512)S(1)}, s32[512]{0:T(512)}, u32[]{:S(2)}) copy-start(s32[512]{0:T(512)} %deg_ref.1) | copy-start | bytes 6148

commit v6 on v5

--- a/solution.py
+++ b/solution.py
@@ -159,7 +159,7 @@
             rest[at, :] = part[:, LANES : 2 * LANES]
         return carry
 
-    lax.fori_loop(0, shells // 2, turn_inverse, 0, unroll=4)
+    lax.fori_loop(0, shells // 2, turn_inverse, 0, unroll=8)
 
     def turn(c):
         copies[c].wait()
@@ -178,7 +178,7 @@
                 t2[at, :] = part[:, 2 * LANES : 3 * LANES]
             return carry
 
-        lax.fori_loop(0, orders // 2, turn_profiles, 0, unroll=4)
+        lax.fori_loop(0, orders // 2, turn_profiles, 0, unroll=8)
 
     pad = jnp.zeros((half - shells, 2 * LANES), BF16)
 
@@ -235,11 +235,16 @@
     def target(i):
         return (me + 1 + i) % members
 
+    def pair_sum(n, j, which):
+        send_ref, from_sib = buffers[n][:2]
+        return send_ref[j, core, which].astype(F32) + from_sib[j, which].astype(F32)
+
     def send_chunk(n):
-        send_ref = buffers[n][0]
-        to_sibling, _, _ = transfers(buffers[n][1:], sem_sets[n], send_ref, place)
-
-        def turn_sums(i, carry):
+        send_ref, _, to_far = buffers[n][:3]
+        to_sibling, to_across, _ = transfers(buffers[n][1:], sem_sets[n], send_ref, place)
+        lag = 2
+
+        def first(i):
             j = target(i)
             parts = []
             for b in range(tiles):
@@ -254,26 +259,23 @@
                 block = [p[g * 2 * mine : (g + 1) * 2 * mine] for p in parts]
                 send_ref[j, g % 2, g // 2] = jnp.concatenate(block, axis=0).astype(BF16)
             to_sibling(j).start()
-            return carry
-
-        lax.fori_loop(0, members, turn_sums, 0, unroll=2)
-
-    def pair_sum(n, j, which):
-        send_ref, from_sib = buffers[n][:2]
-        return send_ref[j, core, which].astype(F32) + from_sib[j, which].astype(F32)
-
-    def second(n):
-        to_sibling, to_across, _ = transfers(buffers[n][1:], sem_sets[n], buffers[n][0], place)
-        to_far = buffers[n][2]
-
-        def step(i, carry):
+
+        def second(i):
             j = target(i)
             to_sibling(j).wait_recv()
             to_far[j] = pair_sum(n, j, 1 - y).astype(BF16)
             to_across(j).start()
-            return carry
-
-        lax.fori_loop(0, members, step, 0)
+
+        def step(i, carry):
+            first(i + lag)
+            second(i)
+            return carry
+
+        for i in range(lag):
+            first(i)
+        lax.fori_loop(0, members - lag, step, 0)
+        for i in range(members - lag, members):
+            second(i)
 
     def third(n):
         _, to_across, to_member = transfers(buffers[n][1:], sem_sets[n], buffers[n][0], place)
@@ -317,8 +319,6 @@
     for n, comps in enumerate(CHUNKS):
         for c in comps:
             turn(c)
-        if n:
-            second(n - 1)
         solve_chunk(comps)
         if n:
             third(n - 1)
@@ -328,7 +328,6 @@
         if n == 0:
             pl.semaphore_wait(barrier, members + 1)
         send_chunk(n)
-    second(last)
     third(last)
     for n in range(len(CHUNKS)):
         finish(n)
@@ -370,7 +369,7 @@
             *[pltpu.SemaphoreType.DMA((members,))] * (6 * len(CHUNKS)),
         ],
         compiler_params=pltpu.CompilerParams(
-            collective_id=0, has_side_effects=True, vmem_limit_bytes=52 * 2**20
+            collective_id=0, has_side_effects=True, vmem_limit_bytes=60 * 2**20
         ),
         name="synthesize",
     )(spec, inv, legendre, degree_list, order_map)

time: 42.2 us -> 40.4 us (0.957)
  Pallas kernels: 39.5 us -> 38.3 us
  local copies, waits for them, and re-layouts: 2.48 us -> 1.82 us
    pallas_call x1, Pallas kernels: 35.8 us -> 34.7 us  [synthesize(): pl.pallas_call(functools.partial(synth_body, groups, members), out_shape=...]
    unnamed x8, local copies, waits for them, and re-layouts: 2.48 us -> 1.82 us
where the time goes in v6:
time: 40.4 us; the launch traced here: 40.2 us
  Pallas kernels  38.3 us (95%)
  local copies, waits for them, and re-layouts  1.82 us (5%)
    pallas_call x1, Pallas kernels, synthesize(): pl.pallas_call(functools.partial(synth_body, groups, members), out_shape=...  34.7 us
    pallas_call x1, Pallas kernels, physical(): pl.pallas_call(functools.partial(physical_body, orders), out_shape=jax.Sh...  3.69 us
    unnamed x8, local copies, waits for them, and re-layouts  1.82 us

profile of v6, /device:TPU:0, one launch (start us, length us, event | category | flops | bytes accessed | tf_op | source)
XLA Modules:
  0.0 40.2 jit_solution(7505026719223399180)
XLA Ops:
  0.0 0.0 copy-start.3
  0.0 0.0 copy-start
  0.0 34.7 %synthesize.1 = (bf16[8,96,128]{2,1,0:T(8,128)(2,1)}, bf16[8,48,128]{2,1,0:T(8,128)(2,1)}) custom-call(bf16[3,2,32,192,128]{4,3,2,1,0:T(8,128)(2,1)} %bitcast.5, bf16[48,192,128]{2,1,0:T(8,128)(2,1)} %bitcast.6, bf16[32,64,128]{2,1,0:T(8,128)(2,1)} %leg_hbm.1, s32[512]{0:T(512)} %deg_ref.1, s32[256]{0:T(256)} %refs_3_.1), custom_call_target="tpu_custom_call" | custom-call | tf_op jit(solution)/shard_map/synthesize/pallas_call | solution.py:354
  34.7 0.0 copy-done.3
  34.7 0.0 copy-done
  34.7 0.0 copy-start.1
  34.7 0.9 %copy-done.1 = bf16[8,96,128]{2,1,0:T(8,128)(2,1)S(1)} copy-done((bf16[8,96,128]{2,1,0:T(8,128)(2,1)S(1)}, bf16[8,96,128]{2,1,0:T(8,128)(2,1)}, u32[]{:S(2)}) %copy-start.1) | copy-done | bytes 196632
  35.6 0.0 copy-start.2
  35.6 0.9 %copy-done.2 = bf16[8,48,128]{2,1,0:T(8,128)(2,1)S(1)} copy-done((bf16[8,48,128]{2,1,0:T(8,128)(2,1)S(1)}, bf16[8,48,128]{2,1,0:T(8,128)(2,1)}, u32[]{:S(2)}) %copy-start.2) | copy-done | bytes 98328
  36.5 3.7 %physical.1 = bf16[3,12,8,1536]{3,2,1,0:T(8,128)(2,1)} custom-call(bf16[8,96,128]{2,1,0:T(8,128)(2,1)S(1)} %copy-done.1, bf16[8,48,128]{2,1,0:T(8,128)(2,1)S(1)} %copy-done.2, bf16[3,12,8,1536]{3,2,1,0:T(8,128)(2,1)S(1)} %bitcast.4, s32[256]{0:T(256)S(1)} %copy-done.3), custom_call_target="tpu_custom_call" | custom-call | tf_op jit(solution)/shard_map/physical/pallas_call | solution.py:462
Async XLA Ops:
  0.0 34.7 %copy-start.3 = (s32[256]{0:T(256)S(1)}, s32[256]{0:T(256)}, u32[]{:S(2)}) copy-start(s32[256]{0:T(256)} %refs_3_.1) | copy-start | bytes 3076
  0.0 34.7 %copy-start = (bf16[3,8,12,1536]{3,1,2,0:T(8,128)(2,1)S(1)}, bf16[3,8,12,1536]{3,1,2,0:T(8,128)(2,1)}, u32[]{:S(2)}) copy-start(bf16[3,8,12,1536]{3,1,2,0:T(8,128)(2,1)} %param.9) | copy-start | bytes 2654212
  34.7 0.9 %copy-start.1 = (bf16[8,96,128]{2,1,0:T(8,128)(2,1)S(1)}, bf16[8,96,128]{2,1,0:T(8,128)(2,1)}, u32[]{:S(2)}) copy-start(bf16[8,96,128]{2,1,0:T(8,128)(2,1)} %get-tuple-element.7.refs_0_) | copy-start | bytes 589828
  35.6 0.9 %copy-start.2 = (bf16[8,48,128]{2,1,0:T(8,128)(2,1)S(1)}, bf16[8,48,128]{2,1,0:T(8,128)(2,1)}, u32[]{:S(2)}) copy-start(bf16[8,48,128]{2,1,0:T(8,128)(2,1)} %get-tuple-element.8.refs_1_) | copy-start | bytes 294916

commit v7 on v6

--- a/solution.py
+++ b/solution.py
@@ -135,10 +135,18 @@
             barrier, inc=1, device_id=(grp, (me + i) % members), device_id_type=MESH
         )
 
-    inv_copy = pltpu.make_async_copy(inv_hbm, inv, sems.at[3])
-    inv_copy.start()
+    pieces = 3 if shells % 6 == 0 else 1
+    piece = shells // pieces
+    inv_copies = [
+        pltpu.make_async_copy(
+            inv_hbm.at[pl.ds(i * piece, piece)], inv.at[pl.ds(i * piece, piece)], sems.at[4 + i]
+        )
+        for i in range(pieces)
+    ]
+    for copy in inv_copies:
+        copy.start()
     copies = [pltpu.make_async_copy(spec_hbm.at[c], spec.at[c], sems.at[c]) for c in range(3)]
-    leg_copy = pltpu.make_async_copy(leg_hbm, leg_ref, sems.at[4])
+    leg_copy = pltpu.make_async_copy(leg_hbm, leg_ref, sems.at[3])
     for copy in (*copies, leg_copy):
         copy.start()
 
@@ -146,8 +154,6 @@
         lax.broadcasted_iota(jnp.int32, (2 * width, 2 * width), 0)
         == lax.broadcasted_iota(jnp.int32, (2 * width, 2 * width), 1)
     ).astype(BF16)
-
-    inv_copy.wait()
 
     def turn_inverse(i, carry):
         both = jnp.concatenate([inv[2 * i], inv[2 * i + 1]], axis=1)
@@ -159,26 +165,32 @@
             rest[at, :] = part[:, LANES : 2 * LANES]
         return carry
 
-    lax.fori_loop(0, shells // 2, turn_inverse, 0, unroll=8)
+    for i, copy in enumerate(inv_copies):
+        copy.wait()
+        lax.fori_loop(i * piece // 2, (i + 1) * piece // 2, turn_inverse, 0, unroll=8)
 
     def turn(c):
         copies[c].wait()
 
         def turn_profiles(i, carry):
-            a, b = [
-                jnp.concatenate([spec[c, k, 2 * i], spec[c, k, 2 * i + 1]], axis=1)
-                for k in range(2)
-            ]
-            out = nt(eye, jnp.concatenate([a, b[LANES:], b[:LANES]], axis=0))
-            for h in range(2):
-                at = pl.ds((c * orders + 2 * i + h) * pitch, width)
-                part = out[h * width : (h + 1) * width]
-                t0[at, :] = part[:, 0:LANES]
-                t1[at, :] = part[:, LANES : 2 * LANES]
-                t2[at, :] = part[:, 2 * LANES : 3 * LANES]
-            return carry
-
-        lax.fori_loop(0, orders // 2, turn_profiles, 0, unroll=8)
+            stack = []
+            for p in range(2):
+                m = 4 * i + 2 * p
+                a, b = [
+                    jnp.concatenate([spec[c, k, m], spec[c, k, m + 1]], axis=1)
+                    for k in range(2)
+                ]
+                stack += [a, b[LANES:], b[:LANES]]
+            out = nt(eye, jnp.concatenate(stack, axis=0))
+            for p in range(2):
+                for h in range(2):
+                    at = pl.ds((c * orders + 4 * i + 2 * p + h) * pitch, width)
+                    part = out[h * width : (h + 1) * width]
+                    for n, to in enumerate((t0, t1, t2)):
+                        to[at, :] = part[:, (3 * p + n) * LANES : (3 * p + n + 1) * LANES]
+            return carry
+
+        lax.fori_loop(0, orders // 4, turn_profiles, 0, unroll=4)
 
     pad = jnp.zeros((half - shells, 2 * LANES), BF16)
 
@@ -364,7 +376,7 @@
             *[pltpu.VMEM((shells * pitch, LANES), F32)] * 2,
             pltpu.VMEM((3 * orders * pitch, LANES), F32),
             *[pltpu.VMEM((lats * (orders + 1), LANES), F32)] * 3,
-            pltpu.SemaphoreType.DMA((5,)),
+            pltpu.SemaphoreType.DMA((7,)),
             *buffers,
             *[pltpu.SemaphoreType.DMA((members,))] * (6 * len(CHUNKS)),
         ],
@@ -470,7 +482,7 @@
         ]
         + [pltpu.VMEM(r.shape, BF16) for r in received]
         + [pltpu.VMEM((3 * shells * lats, LANES), F32)] * (2 * members * orders // LANES),
-        compiler_params=pltpu.CompilerParams(vmem_limit_bytes=24 * 2**20),
+        compiler_params=pltpu.CompilerParams(vmem_limit_bytes=60 * 2**20),
         name="physical",
     )(*received, vorticity, order_map)
 
@@ -499,7 +511,7 @@
             and LANES < radii
             and 2 * radii == 3 * LANES
             and LANES % orders == 0
-            and orders % 2 == 0
+            and orders % 4 == 0
             and shells % 2 == 0
             and (shells // groups * 2) % 8 == 0
             and members % (LANES // orders) == 0

time: 40.4 us -> 38.1 us (0.943)
  local copies, waits for them, and re-layouts: 1.82 us -> 0 us
    unnamed x8 -> x0, local copies, waits for them, and re-layouts: 1.82 us -> none
    pallas_call x1, Pallas kernels: 34.7 us -> 33.5 us  [synthesize(): pl.pallas_call(functools.partial(synth_body, groups, members), out_shape=...]
    pallas_call x1, Pallas kernels: 3.69 us -> 4.37 us  [physical(): pl.pallas_call(functools.partial(physical_body, orders), out_shape=jax.Sh...]
where the time goes in v7:
time: 38.1 us; the launch traced here: 37.9 us
  Pallas kernels  37.9 us (99%)
    pallas_call x1, Pallas kernels, synthesize(): pl.pallas_call(functools.partial(synth_body, groups, members), out_shape=...  33.5 us
    pallas_call x1, Pallas kernels, physical(): pl.pallas_call(functools.partial(physical_body, orders), out_shape=jax.Sh...  4.37 us

profile of v7, /device:TPU:0, one launch (start us, length us, event | category | flops | bytes accessed | tf_op | source)
XLA Modules:
  0.0 37.9 jit_solution(735634940825982069)
XLA Ops:
  0.0 33.5 %synthesize.1 = (bf16[8,96,128]{2,1,0:T(8,128)(2,1)}, bf16[8,48,128]{2,1,0:T(8,128)(2,1)}) custom-call(bf16[3,2,32,192,128]{4,3,2,1,0:T(8,128)(2,1)} %bitcast.4, bf16[48,192,128]{2,1,0:T(8,128)(2,1)} %bitcast.5, bf16[32,64,128]{2,1,0:T(8,128)(2,1)} %leg_hbm.1, s32[512]{0:T(512)} %deg_ref.1, s32[256]{0:T(256)} %refs_3_.1), custom_call_target="tpu_custom_call" | custom-call | tf_op jit(solution)/shard_map/synthesize/pallas_call | solution.py:366
  33.6 4.4 %physical.1 = bf16[3,12,8,1536]{3,2,1,0:T(8,128)(2,1)} custom-call(bf16[8,96,128]{2,1,0:T(8,128)(2,1)} %get-tuple-element.7.refs_0_, bf16[8,48,128]{2,1,0:T(8,128)(2,1)} %get-tuple-element.8.refs_1_, bf16[3,12,8,1536]{3,2,1,0:T(8,128)(2,1)} %bitcast.6, s32[256]{0:T(256)} %refs_3_.1), custom_call_target="tpu_custom_call" | custom-call | tf_op jit(solution)/shard_map/physical/pallas_call | solution.py:474

commit v8 on v7

--- a/solution.py
+++ b/solution.py
@@ -332,11 +332,11 @@
         for c in comps:
             turn(c)
         solve_chunk(comps)
-        if n:
-            third(n - 1)
         if n == 0:
             leg_copy.wait()
         sum_chunk(comps)
+        if n:
+            third(n - 1)
         if n == 0:
             pl.semaphore_wait(barrier, members + 1)
         send_chunk(n)
@@ -403,9 +403,9 @@
     return cos, sin
 
 
-def physical_body(orders, *refs):
+def physical_body(orders, wide, *refs):
     recvs, refs = refs[: len(CHUNKS)], refs[len(CHUNKS) :]
-    vort_hbm, ord_ref, out_ref, vort_ref, sem, *keep = refs
+    vort_hbm, ord_ref, out_hbm, vort_ref, made, sem, *keep = refs
     held, keep = keep[: len(CHUNKS)], keep[len(CHUNKS) :]
     copy = pltpu.make_async_copy(vort_hbm, vort_ref, sem.at[0])
     arrivals = [
@@ -453,32 +453,45 @@
     left = jnp.concatenate([r[...].astype(BF16) for r in keep], axis=1)
 
     flat = shells * lats
+    shape = (shells, lats, wide)
     copy.wait()
-    for q in range(points // LANES):
-        on = slice(q * LANES, (q + 1) * LANES)
-        fc, fs = far_c[:, q : q + 1], far_s[:, q : q + 1]
-        trig = jnp.concatenate([nc * fc - ns * fs, -(ns * fc + nc * fs)], axis=0).astype(BF16)
-        v = nn(left, trig)
+    writes = []
+    for q in range(points // wide):
+        on = pl.ds(q * wide, wide)
+        tables = []
+        for p in range(q * wide // LANES, (q + 1) * wide // LANES):
+            fc, fs = far_c[:, p : p + 1], far_s[:, p : p + 1]
+            tables.append(jnp.concatenate([nc * fc - ns * fs, -(ns * fc + nc * fs)], axis=0))
+        v = nn(left, jnp.concatenate(tables, axis=1).astype(BF16))
         v0, v1, v2 = v[:flat], v[flat : 2 * flat], v[2 * flat :]
-        w0, w1, w2 = [vort_ref[c, :, :, on].reshape(flat, LANES).astype(F32) for c in range(3)]
-        shape = (shells, lats, LANES)
-        out_ref[0, :, :, on] = (v1 * w2 - v2 * w1).astype(BF16).reshape(shape)
-        out_ref[1, :, :, on] = (v2 * w0 - v0 * w2).astype(BF16).reshape(shape)
-        out_ref[2, :, :, on] = (v0 * w1 - v1 * w0).astype(BF16).reshape(shape)
+        w0, w1, w2 = [vort_ref[c, :, :, on].reshape(flat, wide).astype(F32) for c in range(3)]
+        made[0, :, :, on] = (v1 * w2 - v2 * w1).astype(BF16).reshape(shape)
+        made[1, :, :, on] = (v2 * w0 - v0 * w2).astype(BF16).reshape(shape)
+        made[2, :, :, on] = (v0 * w1 - v1 * w0).astype(BF16).reshape(shape)
+        writes.append(
+            pltpu.make_async_copy(
+                made.at[:, :, :, on], out_hbm.at[:, :, :, on], sem.at[1 + len(CHUNKS) + q]
+            )
+        )
+        writes[-1].start()
+    for write in writes:
+        write.wait()
 
 
 def physical(received, vorticity, order_map, orders):
     members = received[0].shape[0]
-    _, shells, lats, _ = vorticity.shape
+    _, shells, lats, points = vorticity.shape
+    wide = 2 * LANES if points % (2 * LANES) == 0 else LANES
     vmem = pl.BlockSpec(memory_space=pltpu.VMEM)
     return pl.pallas_call(
-        functools.partial(physical_body, orders),
+        functools.partial(physical_body, orders, wide),
         out_shape=jax.ShapeDtypeStruct(vorticity.shape, BF16),
         in_specs=[pl.BlockSpec(memory_space=pl.ANY)] * (len(CHUNKS) + 1) + [vmem],
-        out_specs=vmem,
+        out_specs=pl.BlockSpec(memory_space=pl.ANY),
         scratch_shapes=[
             pltpu.VMEM(vorticity.shape, BF16),
-            pltpu.SemaphoreType.DMA((1 + len(CHUNKS),)),
+            pltpu.VMEM(vorticity.shape, BF16),
+            pltpu.SemaphoreType.DMA((1 + len(CHUNKS) + points // wide,)),
         ]
         + [pltpu.VMEM(r.shape, BF16) for r in received]
         + [pltpu.VMEM((3 * shells * lats, LANES), F32)] * (2 * members * orders // LANES),

time: 38.1 us -> 38 us (level)
  no operation moved by 1% of the time
where the time goes in v8:
time: 38 us; the launch traced here: 37.8 us
  Pallas kernels  37.8 us (99%)
    pallas_call x1, Pallas kernels, synthesize(): pl.pallas_call(functools.partial(synth_body, groups, members), out_shape=...  33.6 us
    pallas_call x1, Pallas kernels, physical(): pl.pallas_call(functools.partial(physical_body, orders, wide), out_shape=...  4.24 us

profile of v8, /device:TPU:0, one launch (start us, length us, event | category | flops | bytes accessed | tf_op | source)
XLA Modules:
  0.0 37.8 jit_solution(713242536821367657)
XLA Ops:
  0.0 33.6 %synthesize.1 = (bf16[8,96,128]{2,1,0:T(8,128)(2,1)}, bf16[8,48,128]{2,1,0:T(8,128)(2,1)}) custom-call(bf16[3,2,32,192,128]{4,3,2,1,0:T(8,128)(2,1)} %bitcast.4, bf16[48,192,128]{2,1,0:T(8,128)(2,1)} %bitcast.5, bf16[32,64,128]{2,1,0:T(8,128)(2,1)} %leg_hbm.1, s32[512]{0:T(512)} %deg_ref.1, s32[256]{0:T(256)} %refs_3_.1), custom_call_target="tpu_custom_call" | custom-call | tf_op jit(solution)/shard_map/synthesize/pallas_call | solution.py:366
  33.6 4.2 %physical.1 = bf16[3,12,8,1536]{3,2,1,0:T(8,128)(2,1)} custom-call(bf16[8,96,128]{2,1,0:T(8,128)(2,1)} %get-tuple-element.7.refs_0_, bf16[8,48,128]{2,1,0:T(8,128)(2,1)} %get-tuple-element.8.refs_1_, bf16[3,12,8,1536]{3,2,1,0:T(8,128)(2,1)} %bitcast.6, s32[256]{0:T(256)} %refs_3_.1), custom_call_target="tpu_custom_call" | custom-call | tf_op jit(solution)/shard_map/physical/pallas_call | solution.py:486

commit v9 on v8

--- a/solution.py
+++ b/solution.py
@@ -232,7 +232,7 @@
                 sums[c][at, :] = out[:, i * LANES : (i + 1) * LANES]
             return carry
 
-        lax.fori_loop(0, orders, sum_degrees, 0, unroll=8)
+        lax.fori_loop(0, orders, sum_degrees, 0, unroll=16)
 
     row = lax.broadcasted_iota(jnp.int32, (2 * shells, LANES), 0)
     lane = lax.broadcasted_iota(jnp.int32, (2 * shells, LANES), 1)
@@ -332,11 +332,11 @@
         for c in comps:
             turn(c)
         solve_chunk(comps)
+        if n:
+            third(n - 1)
         if n == 0:
             leg_copy.wait()
         sum_chunk(comps)
-        if n:
-            third(n - 1)
         if n == 0:
             pl.semaphore_wait(barrier, members + 1)
         send_chunk(n)

time: 38 us -> 37.4 us (0.984)
  Pallas kernels: 37.8 us -> 37.2 us
    pallas_call x1, Pallas kernels: 33.6 us -> 33 us  [synthesize(): pl.pallas_call(functools.partial(synth_body, groups, members), out_shape=...]
where the time goes in v9:
time: 37.4 us; the launch traced here: 37.2 us
  Pallas kernels  37.2 us (99%)
    pallas_call x1, Pallas kernels, synthesize(): pl.pallas_call(functools.partial(synth_body, groups, members), out_shape=...  33 us
    pallas_call x1, Pallas kernels, physical(): pl.pallas_call(functools.partial(physical_body, orders, wide), out_shape=...  4.24 us

profile of v9, /device:TPU:0, one launch (start us, length us, event | category | flops | bytes accessed | tf_op | source)
XLA Modules:
  0.0 37.2 jit_solution(9758038622097139369)
XLA Ops:
  0.0 33.0 %synthesize.1 = (bf16[8,96,128]{2,1,0:T(8,128)(2,1)}, bf16[8,48,128]{2,1,0:T(8,128)(2,1)}) custom-call(bf16[3,2,32,192,128]{4,3,2,1,0:T(8,128)(2,1)} %bitcast.4, bf16[48,192,128]{2,1,0:T(8,128)(2,1)} %bitcast.5, bf16[32,64,128]{2,1,0:T(8,128)(2,1)} %leg_hbm.1, s32[512]{0:T(512)} %deg_ref.1, s32[256]{0:T(256)} %refs_3_.1), custom_call_target="tpu_custom_call" | custom-call | tf_op jit(solution)/shard_map/synthesize/pallas_call | solution.py:366
  33.0 4.2 %physical.1 = bf16[3,12,8,1536]{3,2,1,0:T(8,128)(2,1)} custom-call(bf16[8,96,128]{2,1,0:T(8,128)(2,1)} %get-tuple-element.7.refs_0_, bf16[8,48,128]{2,1,0:T(8,128)(2,1)} %get-tuple-element.8.refs_1_, bf16[3,12,8,1536]{3,2,1,0:T(8,128)(2,1)} %bitcast.6, s32[256]{0:T(256)} %refs_3_.1), custom_call_target="tpu_custom_call" | custom-call | tf_op jit(solution)/shard_map/physical/pallas_call | solution.py:486
